TPU v7x, 768 devices: a whole 4x8x12 slice. The times are simulated.
768 devices in a mesh: row: 24 (over x_lo, z), col: 32 (over x_hi, y, core).
Axes of the slice: x: 4 (x_hi: 2, x_lo: 2; x = x_hi * 2 + x_lo), y: 8, z: 12, core: 2. Of those that a mesh axis runs over, the one named last changes fastest.
Arguments:
- features: bfloat16 [98304, 128], P(('row', 'col')), may hold values from -6 to 6
- deg_scale: bfloat16 [98304], P(('row', 'col')), may hold values from 0.049804688 to 0.5
- weight: bfloat16 [128, 256], replicated, may hold values from -0.5 to 0.5
- cotangent: bfloat16 [98304, 256], P(('row', 'col')), may hold values from -6 to 6
- tile_rows: int32 [24, 32, 48], P('row', 'col'), may hold values from 0 to 15, as said below
- tile_cols: int32 [24, 32, 48], P('row', 'col'), may hold values from 0 to 11, as said below
- tile_count: int32 [24, 32], P('row', 'col'), may hold values from 6 to 48, as said below
- tile_bits: int32 [24, 32, 48, 32, 256], P('row', 'col'), may hold values from 0 to 255, as said below
Outputs:
- activations: bfloat16 [98304, 256], P(('row', 'col'))
- input_grad: bfloat16 [98304, 128], P(('row', 'col'))
- weight_grad: float32 [128, 256], replicated
Inputs may be any that keep to these rules, and one draw needn't show every extreme that they name: The 48 slots of one block name distinct pairs (tile_rows, tile_cols). `tile_cols`: paired with tile_rows slot by slot. `tile_count`: some block fills all 48 slots. `tile_bits`: bit k of word [a, b] of a slot is the tile's entry in row 8 a + k and column b.
All inputs are finite; a program needn't handle non-finite values.
Results may differ from a plain program's by a relative error of at most 0.0065.
Values may be sent and summed in bfloat16 or wider, within the bound.
A program may use at most 32 MiB of HBM per device.

v0:
```python
import math

import jax
import jax.numpy as jnp
from jax import lax
from jax.sharding import PartitionSpec as P


def unpack_tiles(packed):
    shifts = jnp.arange(8, dtype=jnp.int32)
    bit_values = jnp.bitwise_and(
        jnp.right_shift(packed[:, :, None, :], shifts[None, None, :, None]), 1
    )
    return bit_values.reshape(packed.shape[0], packed.shape[1] * 8, packed.shape[2]).astype(
        jnp.bfloat16
    )


def silu_slope(pre_act):
    sigmoid_value = jax.nn.sigmoid(pre_act)
    return sigmoid_value * (1.0 + pre_act * (1.0 - sigmoid_value))


def accumulate(source, packed, pick_ids, place_ids, live_count, places, forward, turn_count):
    per_block = 8
    feature_width = source.shape[-1]
    tile_size = packed.shape[-1]
    slot_ids = jnp.arange(per_block, dtype=jnp.int32)
    targets = jnp.arange(places, dtype=jnp.int32)

    def block_step(step_index, running):
        first_slot = step_index * per_block
        mask_tiles = unpack_tiles(lax.dynamic_slice_in_dim(packed, first_slot, per_block, 0))
        picked = jnp.take(
            source, lax.dynamic_slice_in_dim(pick_ids, first_slot, per_block, 0), axis=0
        )
        if forward:
            products = jnp.einsum(
                "sab,sbf->saf", mask_tiles, picked, preferred_element_type=jnp.float32
            )
        else:
            products = jnp.einsum(
                "sab,saf->sbf", mask_tiles, picked, preferred_element_type=jnp.float32
            )
        live_slots = (first_slot + slot_ids < live_count).astype(jnp.float32)
        chosen = lax.dynamic_slice_in_dim(place_ids, first_slot, per_block, 0)
        onehot = (chosen[None, :] == targets[:, None]).astype(jnp.float32) * live_slots[None, :]
        flat_products = products.reshape(per_block, tile_size * feature_width)
        return running + jnp.dot(
            onehot,
            flat_products,
            precision=lax.Precision.HIGHEST,
            preferred_element_type=jnp.float32,
        )

    initial = jnp.zeros((places, tile_size * feature_width), jnp.float32)
    running = lax.fori_loop(0, turn_count, block_step, initial)
    return running.reshape(places * tile_size, feature_width)


def on_device(features, deg_scale, weight, cotangent, tile_rows, tile_cols, tile_count, tile_bits):
    row_index = tile_rows[0, 0]
    col_index = tile_cols[0, 0]
    live_count = tile_count[0, 0]
    packed = tile_bits[0, 0]
    tile_size = packed.shape[-1]
    feature_width = features.shape[1]
    vertices = features.shape[0]
    row_shards = lax.axis_size("row")
    col_shards = lax.axis_size("col")
    row_tiles = col_shards * vertices // tile_size
    col_tiles = row_shards * vertices // tile_size
    total_verts = vertices * row_shards * col_shards
    turn_count = packed.shape[0] // 8
    scale = deg_scale.astype(jnp.float32)
    scaled = (features.astype(jnp.float32) * scale[:, None]).astype(jnp.bfloat16)
    column_block = lax.all_gather(scaled, "row", axis=0, tiled=True).reshape(
        col_tiles, tile_size, feature_width
    )
    partial_value = accumulate(
        column_block, packed, col_index, row_index, live_count, row_tiles, True, turn_count
    )
    summed = lax.psum_scatter(partial_value, "col", scatter_dimension=0, tiled=True)
    hidden = (summed * scale[:, None]).astype(jnp.bfloat16)
    pre_act = jnp.dot(hidden, weight, preferred_element_type=jnp.float32)
    activations = jax.nn.silu(pre_act).astype(jnp.bfloat16)
    slope_term = (cotangent.astype(jnp.float32) * silu_slope(pre_act)).astype(jnp.bfloat16)
    local_grad = lax.dot_general(
        hidden, slope_term, (((0,), (0,)), ((), ())), preferred_element_type=jnp.float32
    )
    weight_grad = lax.psum(local_grad, ("row", "col")) / math.sqrt(total_verts)
    spread = lax.dot_general(
        slope_term, weight, (((1,), (1,)), ((), ())), preferred_element_type=jnp.float32
    )
    back = (spread * scale[:, None]).astype(jnp.bfloat16)
    row_block = lax.all_gather(back, "col", axis=0, tiled=True)
    sources = row_block.reshape(row_tiles, tile_size, feature_width)
    partial_back = accumulate(
        sources, packed, row_index, col_index, live_count, col_tiles, False, turn_count
    )
    gathered_back = lax.psum_scatter(partial_back, "row", scatter_dimension=0, tiled=True)
    input_grad = (gathered_back * scale[:, None]).astype(jnp.bfloat16)
    return (activations, input_grad, weight_grad)


def solution(mesh):
    in_specs = (
        P(("row", "col"), None),
        P(("row", "col")),
        P(),
        P(("row", "col"), None),
        P("row", "col", None),
        P("row", "col", None),
        P("row", "col"),
        P("row", "col", None, None, None),
    )
    out_specs = (P(("row", "col"), None), P(("row", "col"), None), P())
    return jax.shard_map(
        on_device, mesh=mesh, in_specs=in_specs, out_specs=out_specs, check_vma=False
    )
```

profile of v0, /device:TPU:1, one launch (start us, length us, event | category | flops | bytes accessed | tf_op | source)
XLA Modules:
  0.0 915.8 jit_solution(15481668004733191987)
XLA Ops:
  8.7 55.6 %all_gather.6 = bf16[3072,128]{1,0:T(8,128)(2,1)} all-gather(bf16[128,128]{1,0:T(8,128)(2,1)S(1)} %multiply_convert_fusion.4), channel_id=1, replica_groups=mesh['row'=24,'col'=32] {'row'}, dimensions={0}, use_global_device_ids=true | all-gather | bytes 819200 | tf_op jit(solution)/shard_map/all_gather | solution.py:77
  64.3 59.2 %while.28 = (s32[]{:T(128)}, f32[16,32768]{1,0:T(8,128)S(1)}, s32[48]{0:T(128)}, s32[]{:T(128)}, s32[48,32,256]{2,1,0:T(8,128)}, /*index=5*/s32[48]{0:T(128)}, b...) while((s32[]{:T(128)}, f32[16,32768]{1,0:T(8,128)S(1)}, ...), condition=%wide.region_1.0_spmd.clone, body=%wide.region_0.1_spmd.clone.sunk | while | flops 187434320 | bytes 8660237 | solution.py:57
  66.8 2.6 gather_fusion
  71.0 3.2 convolution_add_fusion.4
  76.7 2.6 gather_fusion
  80.9 3.2 convolution_add_fusion.4
  86.6 2.6 gather_fusion
  90.8 3.2 convolution_add_fusion.4
  96.4 2.6 gather_fusion
  100.6 3.2 convolution_add_fusion.4
  106.3 2.6 gather_fusion
  110.5 3.2 convolution_add_fusion.4
  116.2 2.6 gather_fusion
  120.4 3.2 convolution_add_fusion.4
  125.1 134.6 %reduce-scatter.3.cloned.1.call-done = f32[128,128]{1,0:T(8,128)} async-done(((f32[4096,128]{1,0:T(8,128)}), f32[128,128]{1,0:T(8,128)}) %reduce-scatter.3.cloned.1.call-update) | async-done | bytes 65552 | tf_op jit(solution)/shard_map/reduce_scatter | solution.py:83
  262.3 1.8 fusion.45
  264.1 93.1 %all-gather.2.cloned.1.call-done = bf16[4096,128]{1,0:T(8,128)(2,1)} async-done(((bf16[128,128]{1,0:T(8,128)(2,1)}), bf16[4096,128]{1,0:T(8,128)(2,1)}) %all-gather.2.cloned.1.call-update) | async-done | bytes 1048592 | tf_op jit(solution)/shard_map/all_gather | solution.py:96
  357.3 56.6 %while.29 = (s32[]{:T(128)}, f32[12,32768]{1,0:T(8,128)S(1)}, s32[48]{0:T(128)S(1)}, s32[]{:T(128)}, s32[48,32,256]{2,1,0:T(8,128)}, /*index=5*/s32[48]{0:T(128)...) while((s32[]{:T(128)}, f32[12,32768]{1,0:T(8,128)S(1)}, ...), condition=%wide.region_4.5_spmd.clone, body=%wide.region_3.4_spmd.clone.sunk | while | flops 174589200 | bytes 7610865 | solution.py:57
  359.1 2.7 gather_fusion.1
  363.5 3.2 convolution_add_fusion.5
  368.5 2.7 gather_fusion.1
  372.9 3.2 convolution_add_fusion.5
  377.9 2.7 gather_fusion.1
  382.4 3.2 convolution_add_fusion.5
  387.4 2.7 gather_fusion.1
  391.8 3.2 convolution_add_fusion.5
  396.8 2.7 gather_fusion.1
  401.2 3.2 convolution_add_fusion.5
  406.2 2.7 gather_fusion.1
  410.7 3.2 convolution_add_fusion.5
  415.2 401.9 %all-reduce.2.cloned.1.call-done = f32[128,256]{1,0:T(8,128)} async-done(((f32[128,256]{1,0:T(8,128)}), f32[128,256]{1,0:T(8,128)}) %all-reduce.2.cloned.1.call-update) | async-done | bytes 131088 | tf_op jit(solution)/shard_map/psum | solution.py:91
  818.7 89.0 %reduce-scatter.5.cloned.1.call-done = f32[128,128]{1,0:T(8,128)} async-done(((f32[3072,128]{1,0:T(8,128)}), f32[128,128]{1,0:T(8,128)}) %reduce-scatter.5.cloned.1.call-update) | async-done | bytes 65552 | tf_op jit(solution)/shard_map/reduce_scatter | solution.py:101
  (122 shorter events, 56.0 us)
Async XLA Ops:
  7.2 252.5 %copy-start = (bf16[128,256]{1,0:T(8,128)(2,1)S(1)}, bf16[128,256]{1,0:T(8,128)(2,1)}, u32[]{:S(2)}) copy-start(bf16[128,256]{1,0:T(8,128)(2,1)} %param.14) | copy-start | bytes 196612
  7.2 252.5 %reduce-scatter.3.cloned.1.call-start = ((), (), s32[]{:S(2)}) async-start(), calls=%async_computation.2 | async-start | bytes 2162688 | tf_op jit(solution)/shard_map/reduce_scatter | solution.py:83
  64.4 6.5 copy-start.1
  74.3 6.5 copy-start.1
  84.2 6.5 copy-start.1
  94.0 6.5 copy-start.1
  103.9 6.5 copy-start.1
  113.8 6.5 copy-start.1
  125.0 134.7 %copy-start.4 = (bf16[128,256]{1,0:T(8,128)(2,1)S(1)}, bf16[128,256]{1,0:T(8,128)(2,1)}, u32[]{:S(2)}) copy-start(bf16[128,256]{1,0:T(8,128)(2,1)} %param.15) | copy-start | bytes 196612
  125.0 232.2 %copy-start.2 = (s32[48]{0:T(128)S(1)}, s32[48]{0:T(128)}, u32[]{:S(2)}) copy-start(s32[48]{0:T(128)} %get-tuple-element.593) | copy-start | bytes 580
  125.1 232.2 %copy-start.3 = (s32[48]{0:T(128)S(1)}, s32[48]{0:T(128)}, u32[]{:S(2)}) copy-start(s32[48]{0:T(128)} %get-tuple-element.594) | copy-start | bytes 580
  125.1 232.2 %all-gather.2.cloned.1.call-start = ((), (), s32[]{:S(2)}) async-start(), calls=%async_computation.3 | async-start | bytes 1081344 | tf_op jit(solution)/shard_map/all_gather | solution.py:96
  262.2 554.9 %all-reduce.2.cloned.1.call-start = ((), (), s32[]{:S(2)}) async-start(), calls=%async_computation.5 | async-start | bytes 262144 | tf_op jit(solution)/shard_map/psum | solution.py:91
  264.1 643.6 %reduce-scatter.5.cloned.1.call-start = ((), (), s32[]{:S(2)}) async-start(), calls=%async_computation.4 | async-start | bytes 1638400 | tf_op jit(solution)/shard_map/reduce_scatter | solution.py:101
Sparse Core Ops, SparseCore 0:
  125.2 134.4 reduce-scatter.2
  264.9 92.3 all-gather.1
  364.1 452.9 all-reduce.1
  820.1 87.6 reduce-scatter.4
where the time goes:
time: 934 us; the launch traced here: 916 us
  waiting for transfers between devices  719 us (77%)
  matrix products  61.4 us (7%)
  blocking collectives  55.6 us (6%)
  local copies, waits for them, and re-layouts  48 us (5%)
  other arithmetic  17.3 us (2%)
  between operations  13.8 us (1%)
    psum x1, waiting for transfers between devices, on_device(): weight_grad = lax.psum(local_grad, ('row', 'col')) / math.sqrt(total_verts)  402 us
    reduce_scatter x1, waiting for transfers between devices, on_device(): lax.psum_scatter(partial_value, 'col', scatter_dimension=0, tiled=True)  135 us
    all_gather x1, waiting for transfers between devices, on_device(): row_block = lax.all_gather(back, 'col', axis=0, tiled=True)  93.1 us
    reduce_scatter x1, waiting for transfers between devices, on_device(): lax.psum_scatter(partial_back, 'row', scatter_dimension=0, tiled=True)  89 us
    all_gather x1, blocking collectives, on_device(): lax.all_gather(scaled, 'row', axis=0, tiled=True)  55.6 us
    dot_general x12, matrix products, block_step(): jnp.dot(onehot, flat_products, precision=lax.Precision.HIGHEST, preferred...  37.8 us
    gather x12, local copies, waits for them, and re-layouts, block_step(): jnp.take(source, lax.dynamic_slice_in_dim(pick_ids, first_slot, per_block...  31.4 us
  transfers between devices with their start and end apart: 4, of which 4 were waited for; matrix products, arithmetic and copies ran while one was open for 7% of the time, Pallas kernels for 0%

commit v1 on v0

v1 whole, which is shorter than its diff:
```python
import functools
import math

import jax
import jax.numpy as jnp
from jax import lax
from jax.experimental import pallas as pl
from jax.experimental.pallas import tpu as pltpu
from jax.sharding import PartitionSpec as P

MESH = pl.DeviceIdType.MESH
F32, BF16 = jnp.float32, jnp.bfloat16
X_LO, Z = 2, 12
X_HI, Y, CORES = 2, 8, 2
V = 128
VMEM_BYTES = 40 * 1024 * 1024
WHOLE = pl.BlockSpec(memory_space=pltpu.VMEM)
SCALARS = pl.BlockSpec(memory_space=pltpu.SMEM)


class Place:
    def __init__(self):
        row, col = lax.axis_index("row"), lax.axis_index("col")
        self.row, self.col = row, col
        self.x_lo, self.z = row // Z, row % Z
        self.x_hi, self.y, self.core = col // (Y * CORES), (col // CORES) % Y, col % CORES

    def at(self, x_lo=None, z=None, x_hi=None, y=None, core=None):
        x_lo = self.x_lo if x_lo is None else x_lo
        z = self.z if z is None else z
        x_hi = self.x_hi if x_hi is None else x_hi
        y = self.y if y is None else y
        core = self.core if core is None else core
        return (x_lo * Z + z, (x_hi * Y + y) * CORES + core)


def greet(peers):
    barrier = pltpu.get_barrier_semaphore()
    for peer in peers:
        pl.semaphore_signal(barrier, inc=1, device_id=peer, device_id_type=MESH)
    return lambda: pl.semaphore_wait(barrier, len(peers))


class Wire:
    def __init__(self, send, recv):
        self.send, self.recv, self.used, self.sent = send, recv, 0, []

    def slot(self):
        self.used += 1
        return self.used - 1

    def copy(self, slot, src, dst, to):
        return pltpu.make_async_remote_copy(
            src_ref=src, dst_ref=dst, send_sem=self.send.at[slot], recv_sem=self.recv.at[slot],
            device_id=to, device_id_type=MESH)

    def start(self, slot, src, dst, to):
        copy = self.copy(slot, src, dst, to)
        copy.start()
        self.sent.append(copy)

    def arrived(self, slot, dst, to):
        self.copy(slot, dst, dst, to).wait_recv()

    def finish(self):
        for copy in self.sent:
            copy.wait_send()


def ring_gather(wire, block, pair, pos, n, right, left, partner, landed=None):
    steps = {"right": n // 2, "left": (n - 1) // 2}
    to = {"right": right, "left": left}
    ways = ("right", "left")
    pair_slot = wire.slot()
    slots = {(w, s, p): wire.slot() for w in ways for s in range(steps[w]) for p in (0, 1)}
    which = (pair, 1 - pair)

    def spot(way, step, p):
        shift = step if way == "left" else n - step
        return block(which[p], (pos + shift) % n)

    def tell(way, step, p):
        if landed is not None:
            shift = step if way == "left" else n - step
            landed(which[p], (pos + shift) % n)

    own = block(pair, pos)
    wire.start(pair_slot, own, own, partner)
    for way in ways:
        wire.start(slots[way, 0, 0], own, own, to[way])
    tell("left", 0, 0)
    other = block(1 - pair, pos)
    wire.arrived(pair_slot, other, partner)
    for way in ways:
        wire.start(slots[way, 0, 1], other, other, to[way])
    tell("left", 0, 1)
    yield
    for step in range(1, max(steps.values()) + 1):
        for p in (0, 1):
            here = []
            for way in ways:
                if step <= steps[way]:
                    ref = spot(way, step, p)
                    wire.arrived(slots[way, step - 1, p], ref, to[way])
                    if step < steps[way]:
                        wire.start(slots[way, step, p], ref, ref, to[way])
                    here.append(way)
            for way in here:
                tell(way, step, p)
        yield


def ring_reduce(wire, value, pair, pos, n, right, left, partner, arms, pair_buf, done):
    steps = {"right": n // 2, "left": (n - 1) // 2}
    to = {"right": right, "left": left}
    ways = ("right", "left")
    slots = {(w, s, p): wire.slot() for w in ways for s in range(steps[w]) for p in (0, 1)}
    pair_slot = wire.slot()
    which = (1 - pair, pair)
    arm = lambda way, step, p: arms.at[ways.index(way), step, p]
    stage = arms.at[2]
    for step in range(max(steps.values())):
        for p in (0, 1):
            for way in ways:
                if step >= steps[way]:
                    continue
                far = steps[way] - step
                target = (pos + (far if way == "right" else n - far)) % n
                total = value(which[p], target)
                if step == 0:
                    src = stage.at[ways.index(way), p]
                else:
                    src = arm(way, step - 1, p)
                    wire.arrived(slots[way, step - 1, p], src, to[way])
                    total = total + src[...].astype(F32)
                src[...] = total.astype(BF16)
                wire.start(slots[way, step, p], src, arm(way, step, p), to[way])
        yield
    totals = []
    for p in (0, 1):
        total = value(which[p], pos)
        for way in ways:
            last = arm(way, steps[way] - 1, p)
            wire.arrived(slots[way, steps[way] - 1, p], last, to[way])
            total = total + last[...].astype(F32)
        totals.append(total)
        if p == 0:
            pair_buf[0] = total.astype(BF16)
            wire.start(pair_slot, pair_buf.at[0], pair_buf.at[1], partner)
    yield
    wire.arrived(pair_slot, pair_buf.at[1], partner)
    done(totals[1] + pair_buf[1].astype(F32))


def together(*jobs):
    jobs = list(jobs)
    while jobs:
        for job in list(jobs):
            try:
                next(job)
            except StopIteration:
                jobs.remove(job)


def column_of(row_vector):
    return jnp.transpose(jnp.broadcast_to(row_vector, (V, V)))


def gather_kernel(features, scale, out, send, recv):
    me = Place()
    right, left = me.at(z=(me.z + 1) % Z), me.at(z=(me.z + Z - 1) % Z)
    partner = me.at(x_lo=1 - me.x_lo)
    ready = greet((right, left, partner))
    scaled = features[...].astype(F32) * column_of(scale[...].astype(F32))
    out[me.row] = scaled.astype(BF16)
    ready()
    wire = Wire(send, recv)
    together(ring_gather(
        wire, lambda pair, pos: out.at[pair * Z + pos], me.x_lo, me.z, Z, right, left, partner))
    wire.finish()


def unpack(words):
    parts = []
    for half in (0, 1):
        part = words[16 * half:16 * half + 16]
        for k in range(8):
            parts.append(jnp.bitwise_and(jnp.right_shift(part, k), 1).astype(F32).astype(BF16))
    return jnp.concatenate(parts, axis=0)


UNROLL = 4


def live_tiles(count, bits, body):
    live = count[0]

    def turn(step, _):
        for u in range(UNROLL):
            slot = step * UNROLL + u
            words = jnp.where(slot < live, bits[slot], 0)
            body(slot, unpack(words))
        return 0

    lax.fori_loop(0, (live + UNROLL - 1) // UNROLL, turn, 0)


def forward_kernel(rows, cols, count, source, bits, out, acc):
    acc[...] = jnp.zeros_like(acc)

    def body(slot, mask):
        i = rows[slot]
        acc[i] = acc[i] + jnp.dot(mask, source[cols[slot]], preferred_element_type=F32)

    live_tiles(count, bits, body)
    for i in range(acc.shape[0]):
        for half in (0, 1):
            out[half, i % Y, i // Y] = acc[i, half * V:half * V + V, :].astype(BF16)


def backward_kernel(rows, cols, count, source, bits, act_in, out, act_out, acc):
    acc[...] = jnp.zeros_like(acc)
    act_out[...] = act_in[...]

    def body(slot, mask):
        i, j = rows[slot], cols[slot]
        y, x_hi = i % Y, i // Y
        back = jnp.concatenate([source[0, y, x_hi], source[1, y, x_hi]], axis=1)
        acc[j] = acc[j] + jnp.dot(back, mask, preferred_element_type=F32)

    live_tiles(count, bits, body)
    for j in range(acc.shape[0]):
        for half in (0, 1):
            out[2 * j + half] = acc[j, :, half * V:half * V + V].astype(BF16)


def vertex_kernel(partial, scale, weight, cotangent, act, row_block, piece,
                  core_buf, arms, pair_buf, natural, slope_buf, grad, grad_core, grad_mine, grad_y,
                  grad_x, send, recv):
    me = Place()
    right, left = me.at(y=(me.y + 1) % Y), me.at(y=(me.y + Y - 1) % Y)
    partner, sibling = me.at(x_hi=1 - me.x_hi), me.at(core=1 - me.core)
    y_peers = [me.at(y=(me.y + d) % Y) for d in range(1, Y)]
    ready = greet([partner, sibling] + y_peers)
    wire = Wire(send, recv)

    order = [4, 5, 3, 6, 2, 7, 1, 0]
    core_slots = {d: wire.slot() for d in order}
    ready()
    for d in order:
        t = (me.y + d) % Y
        wire.start(core_slots[d], partial.at[1 - me.core, t], core_buf.at[t], sibling)
    known = set()

    def value_at(distance):
        def value(pair, pos):
            if distance not in known:
                known.add(distance)
                wire.arrived(core_slots[distance], core_buf.at[pos], sibling)
            return partial[me.core, pos, pair].astype(F32) + core_buf[pos, pair].astype(F32)
        return value

    counter = {"calls": 0}
    plan = []
    for step in range(Y // 2):
        for p in (0, 1):
            plan.append(Y // 2 - step)
            if step < (Y - 1) // 2:
                plan.append(Y - ((Y - 1) // 2 - step))
    plan += [0, 0]

    def value(pair, pos):
        distance = plan[counter["calls"]]
        counter["calls"] += 1
        return value_at(distance)(pair, pos)

    scale_row = scale[...].astype(F32)
    scale_col = column_of(scale_row)
    pieces = []
    together(ring_reduce(wire, value, me.x_hi, me.y, Y, right, left, partner, arms, pair_buf,
                         pieces.append))
    summed = pieces[0]
    for k in range(8):
        natural[pl.ds(k, 16, stride=8), :] = summed[16 * k:16 * k + 16]
    hidden = (natural[...] * scale_col).astype(BF16)
    pre_act = jnp.dot(hidden, weight[...], preferred_element_type=F32)
    sigmoid = 1.0 / (1.0 + jnp.exp(-pre_act))
    slope = sigmoid * (1.0 + pre_act * (1.0 - sigmoid))
    slope_term = (cotangent[...].astype(F32) * slope).astype(BF16)
    back = lax.dot_general(weight[...], slope_term, (((1,), (1,)), ((), ())),
                           preferred_element_type=F32)
    back = (back * scale_row).astype(BF16)
    from_v = lax.broadcasted_iota(jnp.int32, (V, V), 0)
    to_v = lax.broadcasted_iota(jnp.int32, (V, V), 1)
    swap = (from_v == 8 * (to_v % 16) + to_v // 16).astype(F32).astype(BF16)
    row_block[me.core, me.y, me.x_hi] = jnp.dot(
        back, swap, preferred_element_type=F32).astype(BF16)

    forwarded = []

    def forward(pair, pos):
        slot = wire.slot()
        wire.start(slot, row_block.at[me.core, pos, pair], row_block.at[me.core, pos, pair], sibling)
        forwarded.append((slot, row_block.at[1 - me.core, pos, pair]))

    def weight_part():
        act[...] = (pre_act * sigmoid).astype(BF16)
        grad[...] = lax.dot_general(hidden, slope_term, (((0,), (0,)), ((), ())),
                                    preferred_element_type=F32).reshape(2, V // 2, 2 * V)
        slot = wire.slot()
        wire.start(slot, grad.at[1 - me.core], grad_core, sibling)
        yield
        wire.arrived(slot, grad_core, sibling)
        grad_mine[...] = (grad[me.core] + grad_core[...]).reshape(Y, V // 16, 2 * V)
        slots = [wire.slot() for _ in y_peers]
        for d, peer in enumerate(y_peers, 1):
            wire.start(slots[d - 1], grad_mine.at[(me.y + d) % Y], grad_y.at[me.y], peer)
        grad_y[me.y] = grad_mine[me.y]
        yield
        for d, peer in enumerate(y_peers, 1):
            wire.arrived(slots[d - 1], grad_y.at[(me.y + Y - d) % Y], peer)
        total = grad_y[0]
        for k in range(1, Y):
            total = total + grad_y[k]
        grad_x[0] = total[:, :V]
        grad_x[1] = total[:, V:]
        slot = wire.slot()
        wire.start(slot, grad_x.at[1 - me.x_hi], grad_x.at[2], partner)
        yield
        wire.arrived(slot, grad_x.at[2], partner)
        piece[...] = grad_x[me.x_hi] + grad_x[2]

    together(
        ring_gather(wire, lambda pair, pos: row_block.at[me.core, pos, pair], me.x_hi, me.y, Y,
                    right, left, partner, forward),
        weight_part())
    for slot, ref in forwarded:
        wire.arrived(slot, ref, sibling)
    wire.finish()


def scatter_kernel(partial, scale, piece, grad_in, weight_grad, arms, pair_buf, lo_buf, z_buf,
                   send, recv):
    me = Place()
    right, left = me.at(z=(me.z + 1) % Z), me.at(z=(me.z + Z - 1) % Z)
    partner, sibling = me.at(x_lo=1 - me.x_lo), me.at(core=1 - me.core)
    x_peer = me.at(x_hi=1 - me.x_hi)
    z_peers = [me.at(z=(me.z + d) % Z) for d in range(1, Z)]
    y_peers = [me.at(y=(me.y + d) % Y) for d in range(1, Y)]
    ready = greet([partner, sibling, x_peer] + z_peers + y_peers)
    wire = Wire(send, recv)
    scale_row = scale[...].astype(F32)
    ready()

    def value(pair, pos):
        return partial[pair * Z + pos].astype(F32)

    def done(total):
        grad_in[...] = jnp.transpose(total * scale_row).astype(BF16)

    def weight_part():
        slot = wire.slot()
        wire.start(slot, piece, lo_buf, partner)
        yield
        wire.arrived(slot, lo_buf, partner)
        z_buf[me.z] = piece[...] + lo_buf[...]
        slots = [wire.slot() for _ in z_peers]
        for d, peer in enumerate(z_peers, 1):
            wire.start(slots[d - 1], z_buf.at[me.z], z_buf.at[me.z], peer)
        yield
        yield
        for d, peer in enumerate(z_peers, 1):
            wire.arrived(slots[d - 1], z_buf.at[(me.z + Z - d) % Z], peer)
        total = z_buf[0]
        for k in range(1, Z):
            total = total + z_buf[k]
        spot = weight_grad.at[me.core, me.y, me.x_hi]
        spot[...] = total / math.sqrt(X_LO * Z * X_HI * Y * CORES * V)
        slot = wire.slot()
        wire.start(slot, spot, spot, x_peer)
        yield
        wire.arrived(slot, weight_grad.at[me.core, me.y, 1 - me.x_hi], x_peer)
        both = weight_grad.at[me.core, me.y]
        slots = [wire.slot() for _ in y_peers]
        for d, peer in enumerate(y_peers, 1):
            wire.start(slots[d - 1], both, both, peer)
        yield
        for d, peer in enumerate(y_peers, 1):
            wire.arrived(slots[d - 1], weight_grad.at[me.core, (me.y + Y - d) % Y], peer)
        slot = wire.slot()
        wire.start(slot, weight_grad.at[me.core], weight_grad.at[me.core], sibling)
        yield
        wire.arrived(slot, weight_grad.at[1 - me.core], sibling)

    together(
        ring_reduce(wire, value, me.x_lo, me.z, Z, right, left, partner, arms, pair_buf, done),
        weight_part())
    wire.finish()


def sems(count):
    return [pltpu.SemaphoreType.DMA((count,)), pltpu.SemaphoreType.DMA((count,))]


def shape(extent, dtype):
    return jax.ShapeDtypeStruct(extent, dtype)


def talking(collective_id):
    return pltpu.CompilerParams(
        collective_id=collective_id, has_side_effects=True, vmem_limit_bytes=VMEM_BYTES)


def gather_call(features, scale):
    return pl.pallas_call(
        gather_kernel,
        out_shape=shape((X_LO * Z, V, V), BF16),
        in_specs=[WHOLE] * 2,
        out_specs=WHOLE,
        scratch_shapes=sems(2 * Z),
        compiler_params=talking(0),
        name="gather_rows",
    )(features, scale)


def forward_call(rows, cols, count, source, bits):
    return pl.pallas_call(
        forward_kernel,
        out_shape=shape((CORES, Y, X_HI, V, V), BF16),
        in_specs=[SCALARS] * 3 + [WHOLE] * 2,
        out_specs=WHOLE,
        scratch_shapes=[pltpu.VMEM((X_HI * Y, 2 * V, V), F32)],
        compiler_params=pltpu.CompilerParams(vmem_limit_bytes=VMEM_BYTES),
        name="forward_tiles",
    )(rows, cols, count, source, bits)


def vertex_call(partial, scale, weight, cotangent):
    return pl.pallas_call(
        vertex_kernel,
        out_shape=(shape((V, 2 * V), BF16), shape((CORES, Y, X_HI, V, V), BF16), shape((8, V), F32)),
        in_specs=[WHOLE] * 4,
        out_specs=(WHOLE,) * 3,
        scratch_shapes=[
            pltpu.VMEM((Y, X_HI, V, V), BF16),
            pltpu.VMEM((3, Y // 2, 2, V, V), BF16),
            pltpu.VMEM((2, V, V), BF16),
            pltpu.VMEM((V, V), F32),
            pltpu.VMEM((V, 2 * V), BF16),
            pltpu.VMEM((2, V // 2, 2 * V), F32),
            pltpu.VMEM((V // 2, 2 * V), F32),
            pltpu.VMEM((Y, 8, 2 * V), F32),
            pltpu.VMEM((Y, 8, 2 * V), F32),
            pltpu.VMEM((3, 8, V), F32),
        ] + sems(64),
        compiler_params=talking(1),
        name="vertex_part",
    )(partial, scale, weight, cotangent)


def backward_call(rows, cols, count, source, bits, act):
    return pl.pallas_call(
        backward_kernel,
        out_shape=(shape((X_LO * Z, V, V), BF16), shape(act.shape, act.dtype)),
        in_specs=[SCALARS] * 3 + [WHOLE] * 3,
        out_specs=(WHOLE,) * 2,
        scratch_shapes=[pltpu.VMEM((X_LO * Z // 2, V, 2 * V), F32)],
        compiler_params=pltpu.CompilerParams(vmem_limit_bytes=VMEM_BYTES),
        name="backward_tiles",
    )(rows, cols, count, source, bits, act)


def scatter_call(partial, scale, piece):
    return pl.pallas_call(
        scatter_kernel,
        out_shape=(shape((V, V), BF16), shape((CORES, Y, X_HI, 8, V), F32)),
        in_specs=[WHOLE] * 3,
        out_specs=(WHOLE,) * 2,
        scratch_shapes=[
            pltpu.VMEM((3, Z // 2, 2, V, V), BF16),
            pltpu.VMEM((2, V, V), BF16),
            pltpu.VMEM((8, V), F32),
            pltpu.VMEM((Z, 8, V), F32),
        ] + sems(56),
        compiler_params=talking(2),
        name="scatter_rows",
    )(partial, scale, piece)


def on_device(features, deg_scale, weight, cotangent, tile_rows, tile_cols, tile_count, tile_bits):
    rows, cols, count, bits = tile_rows[0, 0], tile_cols[0, 0], tile_count[0], tile_bits[0, 0]
    scale = deg_scale.reshape(1, V)
    column_block = gather_call(features, scale)
    partial = forward_call(rows, cols, count, column_block.reshape(Z, 2 * V, V), bits)
    act, row_block, piece = vertex_call(partial, scale, weight, cotangent)
    partial_back, activations = backward_call(rows, cols, count, row_block, bits, act)
    input_grad, grad = scatter_call(partial_back, scale, piece)
    weight_grad = jnp.transpose(grad, (0, 1, 3, 2, 4)).reshape(V, 2 * V)
    return (activations, input_grad, weight_grad)


def solution(mesh):
    in_specs = (
        P(("row", "col"), None),
        P(("row", "col")),
        P(),
        P(("row", "col"), None),
        P("row", "col", None),
        P("row", "col", None),
        P("row", "col"),
        P("row", "col", None, None, None),
    )
    out_specs = (P(("row", "col"), None), P(("row", "col"), None), P())
    return jax.shard_map(
        on_device, mesh=mesh, in_specs=in_specs, out_specs=out_specs, check_vma=False)
```

time: 934 us -> 122 us (0.13); the launches traced: 916 us -> 121 us
  waiting for transfers between devices: 719 us -> 0 us
  Pallas kernels: 0 us -> 114 us
  matrix products: 61.4 us -> 0 us
  blocking collectives: 55.6 us -> 0 us
  local copies, waits for them, and re-layouts: 48 us -> 5.41 us
  other arithmetic: 17.3 us -> 0 us
  between operations: 13.8 us -> 1.38 us
    psum x1 -> x0, waiting for transfers between devices: 402 us -> none  [on_device(): weight_grad = lax.psum(local_grad, ('row', 'col')) / math.sqrt(total_verts)]
    reduce_scatter x2 -> x0, waiting for transfers between devices: 224 us -> none  [the longest x1 135 us: on_device(): lax.psum_scatter(partial_value, 'col', scatter_dimension=0, tiled=True)]
    pallas_call x0 -> x5, Pallas kernels: none -> 114 us  [the longest x1 50.6 us: vertex_call(): pl.pallas_call(vertex_kernel, out_shape=(shape((V, 2 * V), BF16), shape((...]
    all_gather x1 -> x0, waiting for transfers between devices: 93.1 us -> none  [on_device(): row_block = lax.all_gather(back, 'col', axis=0, tiled=True)]
    dot_general x27 -> x0, matrix products: 61.4 us -> none  [the longest x12 37.8 us: block_step(): jnp.dot(onehot, flat_products, precision=lax.Precision.HIGHEST, preferred...]
    all_gather x1 -> x0, blocking collectives: 55.6 us -> none  [on_device(): lax.all_gather(scaled, 'row', axis=0, tiled=True)]
    gather x12 -> x0, local copies, waits for them, and re-layouts: 31.4 us -> none  [block_step(): jnp.take(source, lax.dynamic_slice_in_dim(pick_ids, first_slot, per_block...]
    and x12 -> x0, other arithmetic: 12.7 us -> none  [block_step(): jnp.take(source, lax.dynamic_slice_in_dim(pick_ids, first_slot, per_block...]
  transfers between devices with their start and end apart: 4 -> 0, of which waited for: 4 -> 0; matrix products, arithmetic and copies ran while one was open for 7% -> 0% of each run, Pallas kernels for 0% -> 0%
where the time goes in v1:
time: 122 us; the launch traced here: 121 us
  Pallas kernels  114 us (93%)
  local copies, waits for them, and re-layouts  5.41 us (4%)
  between operations  1.38 us (1%)
    pallas_call x1, Pallas kernels, vertex_call(): pl.pallas_call(vertex_kernel, out_shape=(shape((V, 2 * V), BF16), shape((...  50.6 us
    pallas_call x1, Pallas kernels, scatter_call(): pl.pallas_call(scatter_kernel, out_shape=(shape((V, V), BF16), shape((COR...  30.3 us
    pallas_call x1, Pallas kernels, gather_call(): pl.pallas_call(gather_kernel, out_shape=shape((X_LO * Z, V, V), BF16), in...  29.6 us
    unnamed x22, local copies, waits for them, and re-layouts  5.41 us

profile of v1, /device:TPU:1, one launch (start us, length us, event | category | flops | bytes accessed | tf_op | source)
XLA Modules:
  0.0 121.2 jit_solution(18308108328531026032)
XLA Ops:
  1.3 0.0 copy-start.4
  1.3 0.7 copy-done.4
  2.0 0.0 copy-start.5
  2.0 0.7 copy-done.5
  2.7 29.6 %gather_rows.1 = bf16[24,128,128]{2,1,0:T(8,128)(2,1)S(1)} custom-call(bf16[128,128]{1,0:T(8,128)(2,1)S(1)} %copy-done.4, bf16[1,128]{1,0:T(2,128)(2,1)S(1)} %bitcast.15), custom_call_target="tpu_custom_call" | custom-call | tf_op jit(solution)/shard_map/gather_rows/pallas_call | solution.py:415
  32.3 0.0 copy-start
  32.3 1.4 %copy-done = s32[1,1,48,32,256]{4,3,2,1,0:T(8,128)S(1)} copy-done((s32[1,1,48,32,256]{4,3,2,1,0:T(8,128)S(1)}, s32[1,1,48,32,256]{4,3,2,1,0:T(8,128)}, u32[]{:S(2)}) %copy-start) | copy-done | bytes 1572888
  33.7 0.0 copy-start.7
  33.7 0.7 copy-done.7
  34.3 0.0 copy-start.8
  34.3 0.7 copy-done.8
  35.0 0.0 copy-start.2
  35.0 0.0 copy-start.3
  35.0 0.0 copy-start.6
  35.0 0.0 copy-start.1
  35.0 0.0 copy-start.9
  35.0 1.7 %forward_tiles.1.partial = bf16[2,8,2,128,128]{4,3,2,1,0:T(8,128)(2,1)S(1)} custom-call(s32[48]{0:T(128)S(1)} %bitcast.18, s32[48]{0:T(128)S(1)} %bitcast.20, s32[1]{0:T(128)} %bitcast.9.count, bf16[12,256,128]{2,1,0:T(8,128)(2,1)S(1)} %bitcast.13, s32[48,32,256]{2,1,0:T(8,128)S(1)} %bitcast.11), custom_call_target="tpu_custom_call" | custom-call | tf_op jit(solution)/shard_map/forward_tiles/pallas_call | solution.py:427
  36.7 0.0 copy-done.2
  36.7 0.0 copy-done.3
  36.7 0.0 copy-done.6
  36.7 50.6 %vertex_part.1 = (bf16[128,256]{1,0:T(8,128)(2,1)S(1)}, bf16[2,8,2,128,128]{4,3,2,1,0:T(8,128)(2,1)S(1)}, f32[8,128]{1,0:T(8,128)S(1)}) custom-call(bf16[2,8,2,128,128]{4,3,2,1,0:T(8,128)(2,1)S(1)} %forward_tiles.1.partial, bf16[1,128]{1,0:T(2,128)(2,1)S(1)} %bitcast.16, bf16[128,256]{1,0:T(8,128)(2,1)S(1)} %copy-done.2, bf16[128,256]{1,0:T(8,128)(2,1)S(1)} %copy-done.3), custom_call_target="tpu_custom_call" | custom-call | tf_op jit(solution)/shard_map/vertex_part/pallas_call | solution.py:439
  87.3 0.0 copy-done.1
  87.4 0.0 copy-done.9
  87.4 2.2 %backward_tiles.1 = (bf16[24,128,128]{2,1,0:T(8,128)(2,1)S(1)}, bf16[128,256]{1,0:T(8,128)(2,1)}) custom-call(s32[48]{0:T(128)S(1)} %bitcast.19, s32[48]{0:T(128)S(1)} %bitcast.21, s32[1]{0:T(128)} %bitcast.10.count, bf16[2,8,2,128,128]{4,3,2,1,0:T(8,128)(2,1)S(1)} %get-tuple-element.10.source, s32[48,32,256]{2,1,0:T(8,128)S(1)} %bitcast.12, ...), custom_call_target="tpu_custom_call" | custom-call | tf_op jit(solution)/shard_map/backward_tiles/pallas_call | solution.py:462
  89.6 30.3 %scatter_rows.1 = (bf16[128,128]{1,0:T(8,128)(2,1)S(1)}, f32[2,8,2,8,128]{4,3,2,1,0:T(8,128)S(1)}) custom-call(bf16[24,128,128]{2,1,0:T(8,128)(2,1)S(1)} %get-tuple-element.13.partial, bf16[1,128]{1,0:T(2,128)(2,1)S(1)} %bitcast.17, f32[8,128]{1,0:T(8,128)S(1)} %get-tuple-element.14.piece), custom_call_target="tpu_custom_call" | custom-call | tf_op jit(solution)/shard_map/scatter_rows/pallas_call | solution.py:474
  119.9 0.6 copy.14
  120.5 0.7 copy.15
Async XLA Ops:
  1.3 0.8 copy-start.4
  2.0 0.7 copy-start.5
  32.3 1.4 %copy-start = (s32[1,1,48,32,256]{4,3,2,1,0:T(8,128)S(1)}, s32[1,1,48,32,256]{4,3,2,1,0:T(8,128)}, u32[]{:S(2)}) copy-start(s32[1,1,48,32,256]{4,3,2,1,0:T(8,128)} %param.15) | copy-start | bytes 4718596
  33.7 0.7 copy-start.7
  34.3 0.7 copy-start.8
  35.0 1.7 %copy-start.2 = (bf16[128,256]{1,0:T(8,128)(2,1)S(1)}, bf16[128,256]{1,0:T(8,128)(2,1)}, u32[]{:S(2)}) copy-start(bf16[128,256]{1,0:T(8,128)(2,1)} %weight.1) | copy-start | bytes 196612
  35.0 1.7 %copy-start.3 = (bf16[128,256]{1,0:T(8,128)(2,1)S(1)}, bf16[128,256]{1,0:T(8,128)(2,1)}, u32[]{:S(2)}) copy-start(bf16[128,256]{1,0:T(8,128)(2,1)} %cotangent.1) | copy-start | bytes 196612
  35.0 1.7 %copy-start.6 = (bf16[128]{0:T(256)(128)(2,1)S(1)}, bf16[128]{0:T(256)(128)(2,1)}, u32[]{:S(2)}) copy-start(bf16[128]{0:T(256)(128)(2,1)} %param.9) | copy-start | bytes 772
  35.0 52.4 %copy-start.1 = (s32[1,1,48,32,256]{4,3,2,1,0:T(8,128)S(1)}, s32[1,1,48,32,256]{4,3,2,1,0:T(8,128)}, u32[]{:S(2)}) copy-start(s32[1,1,48,32,256]{4,3,2,1,0:T(8,128)} %param.15) | copy-start | bytes 4718596
  35.0 52.4 %copy-start.9 = (s32[1,1,48]{2,1,0:T(1,128)S(1)}, s32[1,1,48]{2,1,0:T(1,128)}, u32[]{:S(2)}) copy-start(s32[1,1,48]{2,1,0:T(1,128)} %param.13) | copy-start | bytes 580

commit v2 on v1

--- a/solution.py
+++ b/solution.py
@@ -67,89 +67,172 @@
             copy.wait_send()
 
 
-def ring_gather(wire, block, pair, pos, n, right, left, partner, landed=None):
-    steps = {"right": n // 2, "left": (n - 1) // 2}
-    to = {"right": right, "left": left}
-    ways = ("right", "left")
-    pair_slot = wire.slot()
-    slots = {(w, s, p): wire.slot() for w in ways for s in range(steps[w]) for p in (0, 1)}
-    which = (pair, 1 - pair)
-
-    def spot(way, step, p):
-        shift = step if way == "left" else n - step
-        return block(which[p], (pos + shift) % n)
-
-    def tell(way, step, p):
-        if landed is not None:
-            shift = step if way == "left" else n - step
-            landed(which[p], (pos + shift) % n)
-
-    own = block(pair, pos)
-    wire.start(pair_slot, own, own, partner)
-    for way in ways:
-        wire.start(slots[way, 0, 0], own, own, to[way])
-    tell("left", 0, 0)
-    other = block(1 - pair, pos)
-    wire.arrived(pair_slot, other, partner)
-    for way in ways:
-        wire.start(slots[way, 0, 1], other, other, to[way])
-    tell("left", 0, 1)
-    yield
-    for step in range(1, max(steps.values()) + 1):
-        for p in (0, 1):
-            here = []
-            for way in ways:
-                if step <= steps[way]:
-                    ref = spot(way, step, p)
-                    wire.arrived(slots[way, step - 1, p], ref, to[way])
-                    if step < steps[way]:
-                        wire.start(slots[way, step, p], ref, ref, to[way])
-                    here.append(way)
-            for way in here:
-                tell(way, step, p)
-        yield
-
-
-def ring_reduce(wire, value, pair, pos, n, right, left, partner, arms, pair_buf, done):
-    steps = {"right": n // 2, "left": (n - 1) // 2}
-    to = {"right": right, "left": left}
-    ways = ("right", "left")
-    slots = {(w, s, p): wire.slot() for w in ways for s in range(steps[w]) for p in (0, 1)}
-    pair_slot = wire.slot()
-    which = (1 - pair, pair)
-    arm = lambda way, step, p: arms.at[ways.index(way), step, p]
-    stage = arms.at[2]
-    for step in range(max(steps.values())):
-        for p in (0, 1):
-            for way in ways:
-                if step >= steps[way]:
-                    continue
-                far = steps[way] - step
-                target = (pos + (far if way == "right" else n - far)) % n
-                total = value(which[p], target)
-                if step == 0:
-                    src = stage.at[ways.index(way), p]
-                else:
-                    src = arm(way, step - 1, p)
-                    wire.arrived(slots[way, step - 1, p], src, to[way])
-                    total = total + src[...].astype(F32)
-                src[...] = total.astype(BF16)
-                wire.start(slots[way, step, p], src, arm(way, step, p), to[way])
-        yield
-    totals = []
-    for p in (0, 1):
-        total = value(which[p], pos)
-        for way in ways:
-            last = arm(way, steps[way] - 1, p)
-            wire.arrived(slots[way, steps[way] - 1, p], last, to[way])
-            total = total + last[...].astype(F32)
-        totals.append(total)
-        if p == 0:
-            pair_buf[0] = total.astype(BF16)
-            wire.start(pair_slot, pair_buf.at[0], pair_buf.at[1], partner)
-    yield
-    wire.arrived(pair_slot, pair_buf.at[1], partner)
-    done(totals[1] + pair_buf[1].astype(F32))
+def row_gather(wire, me, out):
+    def block(offset, pair=None):
+        return out.at[(me.x_lo if pair is None else pair) * Z + (me.z + offset) % Z]
+
+    def to(offset):
+        return me.at(z=(me.z + offset) % Z)
+
+    partner = me.at(x_lo=1 - me.x_lo)
+    near = {o: wire.slot() for o in (3, 9, 2, 10, 1, 11)}
+    far = {o: wire.slot() for o in (3, 9, 2, 10, 1, 11)}
+    cross = {o: wire.slot() for o in range(Z)}
+
+    def hand_over(offset):
+        wire.start(cross[offset], block(offset), block(offset), partner)
+
+    for o in near:
+        wire.start(near[o], block(0), block(0), to(o))
+    hand_over(0)
+    yield
+    for o in near:
+        source = Z - o
+        wire.arrived(near[o], block(source), to(o))
+        if o in (3, 9):
+            sign = 1 if o == 3 else -1
+            half = block(source).at[pl.ds(0 if o == 3 else V // 2, V // 2)]
+            wire.start(far[o], half, half, to(3 * sign % Z))
+            wire.start(far[2 * sign % Z], block(source), block(source), to(2 * sign % Z))
+            wire.start(far[sign % Z], block(source), block(source), to(sign % Z))
+        hand_over(source)
+    yield
+    for o, source in ((1, 8), (11, 4), (2, 7), (10, 5)):
+        wire.arrived(far[o], block(source), to(o))
+        hand_over(source)
+    wire.arrived(far[3], block(6).at[pl.ds(0, V // 2)], to(3))
+    wire.arrived(far[9], block(6).at[pl.ds(V // 2, V // 2)], to(9))
+    hand_over(6)
+    yield
+    for o in range(Z):
+        wire.arrived(cross[o], block(o, 1 - me.x_lo), partner)
+
+
+def row_reduce(wire, me, partial, cross_buf, ready, relay, final, done):
+    def to(offset):
+        return me.at(z=(me.z + offset) % Z)
+
+    partner = me.at(x_lo=1 - me.x_lo)
+    order = (4, 8, 5, 7, 6, 2, 10, 1, 11, 3, 9, 0)
+    cross = {o: wire.slot() for o in order}
+    for o in order:
+        t = (me.z + o) % Z
+        wire.start(cross[o], partial.at[(1 - me.x_lo) * Z + t], cross_buf.at[t], partner)
+
+    def value(offset):
+        t = (me.z + offset) % Z
+        wire.arrived(cross[offset], cross_buf.at[t], partner)
+        return partial[me.x_lo * Z + t].astype(F32) + cross_buf[t].astype(F32)
+
+    yield
+    relayed = {o: wire.slot() for o in (1, 11, 2, 10, 3, 9)}
+    relay_at = {1: 0, 11: 1, 2: 2, 10: 3, 3: 4, 9: 5}
+    low, high = pl.ds(0, V // 2), pl.ds(V // 2, V // 2)
+    for o, hop in ((4, 1), (8, 11), (5, 2), (7, 10)):
+        ready[o] = value(o).astype(BF16)
+        wire.start(relayed[hop], ready.at[o], relay.at[relay_at[hop]], to(hop))
+    ready[6] = value(6).astype(BF16)
+    for hop, half in ((3, low), (9, high)):
+        wire.start(relayed[hop], ready.at[6, half], relay.at[relay_at[hop], half], to(hop))
+    yield
+    direct = {o: wire.slot() for o in (2, 10, 1, 11, 3, 9)}
+    for o in (2, 10, 1, 11):
+        ready[o] = value(o).astype(BF16)
+        wire.start(direct[o], ready.at[o], final.at[relay_at[o]], to(o))
+    yield
+    for o, hops, half, rest in ((3, (1, 2, 3), low, high), (9, (11, 10, 9), high, low)):
+        total = value(o)
+        for hop in hops[:2]:
+            wire.arrived(relayed[hop], relay.at[relay_at[hop]], to(hop))
+            total = total + relay[relay_at[hop]].astype(F32)
+        last = relay.at[relay_at[hops[2]], half]
+        wire.arrived(relayed[hops[2]], last, to(hops[2]))
+        cut = V // 2
+        top, bottom = total[:cut], total[cut:]
+        if o == 3:
+            top = top + last[...].astype(F32)
+        else:
+            bottom = bottom + last[...].astype(F32)
+        ready[o, low] = top.astype(BF16)
+        ready[o, high] = bottom.astype(BF16)
+        wire.start(direct[o], ready.at[o], final.at[relay_at[o]], to(o))
+    total = value(0)
+    yield
+    for o in (2, 10, 1, 11, 3, 9):
+        wire.arrived(direct[o], final.at[relay_at[o]], to(o))
+        total = total + final[relay_at[o]].astype(F32)
+    done(total)
+
+
+def col_reduce(wire, me, partial, core_buf, cross_out, cross_buf, ready, final, done):
+    sibling, partner = me.at(core=1 - me.core), me.at(x_hi=1 - me.x_hi)
+    order = (4, 5, 3, 6, 2, 7, 1, 0)
+    cores = {o: wire.slot() for o in order}
+    cross = {o: wire.slot() for o in order}
+    direct = {o: wire.slot() for o in order[:-1]}
+    spot = lambda o: (me.y + o) % Y
+    for o in order:
+        wire.start(cores[o], partial.at[1 - me.core, spot(o)], core_buf.at[spot(o)], sibling)
+    for o in order:
+        t = spot(o)
+        wire.arrived(cores[o], core_buf.at[t], sibling)
+        other = partial[me.core, t, 1 - me.x_hi].astype(F32) + core_buf[t, 1 - me.x_hi].astype(F32)
+        cross_out[o] = other.astype(BF16)
+        wire.start(cross[o], cross_out.at[o], cross_buf.at[t], partner)
+
+    def value(o):
+        t = spot(o)
+        wire.arrived(cross[o], cross_buf.at[t], partner)
+        own = partial[me.core, t, me.x_hi].astype(F32) + core_buf[t, me.x_hi].astype(F32)
+        return own + cross_buf[t].astype(F32)
+
+    for o in order[:-1]:
+        ready[o] = value(o).astype(BF16)
+        wire.start(direct[o], ready.at[o], final.at[o], me.at(y=spot(o)))
+    total = value(0)
+    for o in order[:-1]:
+        wire.arrived(direct[o], final.at[o], me.at(y=spot(o)))
+        total = total + final[o].astype(F32)
+    done(total)
+
+
+def col_gather(wire, me, row_block):
+    sibling, partner = me.at(core=1 - me.core), me.at(x_hi=1 - me.x_hi)
+
+    def block(offset, x_hi, core=None):
+        return row_block.at[me.core if core is None else core, (me.y + offset) % Y, x_hi]
+
+    direct = {o: wire.slot() for o in range(1, Y)}
+    cross = {o: wire.slot() for o in range(Y)}
+    mine = {o: wire.slot() for o in range(Y)}
+    theirs = {o: wire.slot() for o in range(Y)}
+    own = block(0, me.x_hi)
+    for o in (4, 3, 5, 2, 6, 1, 7):
+        wire.start(direct[o], own, own, me.at(y=(me.y + o) % Y))
+
+    def hand_over(o):
+        here = block(o, me.x_hi)
+        wire.start(cross[o], here, here, partner)
+        wire.start(mine[o], here, here, sibling)
+
+    hand_over(0)
+    yield
+    for o in (3, 5, 2, 6):
+        wire.arrived(direct[o], block(Y - o, me.x_hi), me.at(y=(me.y + o) % Y))
+        hand_over(Y - o)
+    yield
+    for o in (1, 7, 4):
+        wire.arrived(direct[o], block(Y - o, me.x_hi), me.at(y=(me.y + o) % Y))
+        hand_over(Y - o)
+    yield
+    for o in (0, 5, 3, 6, 2, 7, 1, 4):
+        here = block(o, 1 - me.x_hi)
+        wire.arrived(cross[o], here, partner)
+        wire.start(theirs[o], here, here, sibling)
+    yield
+    for o in range(Y):
+        wire.arrived(mine[o], block(o, me.x_hi, 1 - me.core), sibling)
+        wire.arrived(theirs[o], block(o, 1 - me.x_hi, 1 - me.core), sibling)
 
 
 def together(*jobs):
@@ -168,15 +251,13 @@
 
 def gather_kernel(features, scale, out, send, recv):
     me = Place()
-    right, left = me.at(z=(me.z + 1) % Z), me.at(z=(me.z + Z - 1) % Z)
-    partner = me.at(x_lo=1 - me.x_lo)
-    ready = greet((right, left, partner))
+    peers = [me.at(z=(me.z + d) % Z) for d in (1, 2, 3, 9, 10, 11)]
+    ready = greet(peers + [me.at(x_lo=1 - me.x_lo)])
     scaled = features[...].astype(F32) * column_of(scale[...].astype(F32))
     out[me.row] = scaled.astype(BF16)
     ready()
     wire = Wire(send, recv)
-    together(ring_gather(
-        wire, lambda pair, pos: out.at[pair * Z + pos], me.x_lo, me.z, Z, right, left, partner))
+    together(row_gather(wire, me, out))
     wire.finish()
 
 
@@ -235,50 +316,18 @@
 
 
 def vertex_kernel(partial, scale, weight, cotangent, act, row_block, piece,
-                  core_buf, arms, pair_buf, natural, slope_buf, grad, grad_core, grad_mine, grad_y,
-                  grad_x, send, recv):
+                  core_buf, cross_out, cross_buf, outgoing, final, natural, grad, grad_core, grad_mine,
+                  grad_y, grad_x, send, recv):
     me = Place()
-    right, left = me.at(y=(me.y + 1) % Y), me.at(y=(me.y + Y - 1) % Y)
     partner, sibling = me.at(x_hi=1 - me.x_hi), me.at(core=1 - me.core)
     y_peers = [me.at(y=(me.y + d) % Y) for d in range(1, Y)]
     ready = greet([partner, sibling] + y_peers)
     wire = Wire(send, recv)
-
-    order = [4, 5, 3, 6, 2, 7, 1, 0]
-    core_slots = {d: wire.slot() for d in order}
-    ready()
-    for d in order:
-        t = (me.y + d) % Y
-        wire.start(core_slots[d], partial.at[1 - me.core, t], core_buf.at[t], sibling)
-    known = set()
-
-    def value_at(distance):
-        def value(pair, pos):
-            if distance not in known:
-                known.add(distance)
-                wire.arrived(core_slots[distance], core_buf.at[pos], sibling)
-            return partial[me.core, pos, pair].astype(F32) + core_buf[pos, pair].astype(F32)
-        return value
-
-    counter = {"calls": 0}
-    plan = []
-    for step in range(Y // 2):
-        for p in (0, 1):
-            plan.append(Y // 2 - step)
-            if step < (Y - 1) // 2:
-                plan.append(Y - ((Y - 1) // 2 - step))
-    plan += [0, 0]
-
-    def value(pair, pos):
-        distance = plan[counter["calls"]]
-        counter["calls"] += 1
-        return value_at(distance)(pair, pos)
-
     scale_row = scale[...].astype(F32)
     scale_col = column_of(scale_row)
+    ready()
     pieces = []
-    together(ring_reduce(wire, value, me.x_hi, me.y, Y, right, left, partner, arms, pair_buf,
-                         pieces.append))
+    col_reduce(wire, me, partial, core_buf, cross_out, cross_buf, outgoing, final, pieces.append)
     summed = pieces[0]
     for k in range(8):
         natural[pl.ds(k, 16, stride=8), :] = summed[16 * k:16 * k + 16]
@@ -296,13 +345,6 @@
     row_block[me.core, me.y, me.x_hi] = jnp.dot(
         back, swap, preferred_element_type=F32).astype(BF16)
 
-    forwarded = []
-
-    def forward(pair, pos):
-        slot = wire.slot()
-        wire.start(slot, row_block.at[me.core, pos, pair], row_block.at[me.core, pos, pair], sibling)
-        forwarded.append((slot, row_block.at[1 - me.core, pos, pair]))
-
     def weight_part():
         act[...] = (pre_act * sigmoid).astype(BF16)
         grad[...] = lax.dot_general(hidden, slope_term, (((0,), (0,)), ((), ())),
@@ -330,19 +372,13 @@
         wire.arrived(slot, grad_x.at[2], partner)
         piece[...] = grad_x[me.x_hi] + grad_x[2]
 
-    together(
-        ring_gather(wire, lambda pair, pos: row_block.at[me.core, pos, pair], me.x_hi, me.y, Y,
-                    right, left, partner, forward),
-        weight_part())
-    for slot, ref in forwarded:
-        wire.arrived(slot, ref, sibling)
+    together(col_gather(wire, me, row_block), weight_part())
     wire.finish()
 
 
-def scatter_kernel(partial, scale, piece, grad_in, weight_grad, arms, pair_buf, lo_buf, z_buf,
-                   send, recv):
+def scatter_kernel(partial, scale, piece, grad_in, weight_grad, cross_buf, outgoing, relay, final,
+                   lo_buf, z_buf, send, recv):
     me = Place()
-    right, left = me.at(z=(me.z + 1) % Z), me.at(z=(me.z + Z - 1) % Z)
     partner, sibling = me.at(x_lo=1 - me.x_lo), me.at(core=1 - me.core)
     x_peer = me.at(x_hi=1 - me.x_hi)
     z_peers = [me.at(z=(me.z + d) % Z) for d in range(1, Z)]
@@ -351,9 +387,6 @@
     wire = Wire(send, recv)
     scale_row = scale[...].astype(F32)
     ready()
-
-    def value(pair, pos):
-        return partial[pair * Z + pos].astype(F32)
 
     def done(total):
         grad_in[...] = jnp.transpose(total * scale_row).astype(BF16)
@@ -393,8 +426,8 @@
         wire.arrived(slot, weight_grad.at[1 - me.core], sibling)
 
     together(
-        ring_reduce(wire, value, me.x_lo, me.z, Z, right, left, partner, arms, pair_buf, done),
-        weight_part())
+        weight_part(),
+        row_reduce(wire, me, partial, cross_buf, outgoing, relay, final, done))
     wire.finish()
 
 
@@ -417,7 +450,7 @@
         out_shape=shape((X_LO * Z, V, V), BF16),
         in_specs=[WHOLE] * 2,
         out_specs=WHOLE,
-        scratch_shapes=sems(2 * Z),
+        scratch_shapes=sems(24),
         compiler_params=talking(0),
         name="gather_rows",
     )(features, scale)
@@ -443,10 +476,11 @@
         out_specs=(WHOLE,) * 3,
         scratch_shapes=[
             pltpu.VMEM((Y, X_HI, V, V), BF16),
-            pltpu.VMEM((3, Y // 2, 2, V, V), BF16),
-            pltpu.VMEM((2, V, V), BF16),
+            pltpu.VMEM((Y, V, V), BF16),
+            pltpu.VMEM((Y, V, V), BF16),
+            pltpu.VMEM((Y, V, V), BF16),
+            pltpu.VMEM((Y, V, V), BF16),
             pltpu.VMEM((V, V), F32),
-            pltpu.VMEM((V, 2 * V), BF16),
             pltpu.VMEM((2, V // 2, 2 * V), F32),
             pltpu.VMEM((V // 2, 2 * V), F32),
             pltpu.VMEM((Y, 8, 2 * V), F32),
@@ -477,8 +511,10 @@
         in_specs=[WHOLE] * 3,
         out_specs=(WHOLE,) * 2,
         scratch_shapes=[
-            pltpu.VMEM((3, Z // 2, 2, V, V), BF16),
-            pltpu.VMEM((2, V, V), BF16),
+            pltpu.VMEM((Z, V, V), BF16),
+            pltpu.VMEM((Z, V, V), BF16),
+            pltpu.VMEM((6, V, V), BF16),
+            pltpu.VMEM((6, V, V), BF16),
             pltpu.VMEM((8, V), F32),
             pltpu.VMEM((Z, 8, V), F32),
         ] + sems(56),

time: 122 us -> 108 us (0.89)
  Pallas kernels: 114 us -> 101 us
    pallas_call x1, Pallas kernels: 50.6 us -> 40 us  [vertex_call(): pl.pallas_call(vertex_kernel, out_shape=(shape((V, 2 * V), BF16), shape((...]
    pallas_call x1, Pallas kernels: 29.6 us -> 27 us  [gather_call(): pl.pallas_call(gather_kernel, out_shape=shape((X_LO * Z, V, V), BF16), in...]
where the time goes in v2:
time: 108 us
  Pallas kernels  101 us (94%)
  local copies, waits for them, and re-layouts  5.41 us (5%)
  between operations  1.38 us (1%)
    pallas_call x1, Pallas kernels, vertex_call(): pl.pallas_call(vertex_kernel, out_shape=(shape((V, 2 * V), BF16), shape((...  40 us
    pallas_call x1, Pallas kernels, scatter_call(): pl.pallas_call(scatter_kernel, out_shape=(shape((V, V), BF16), shape((COR...  30.2 us
    pallas_call x1, Pallas kernels, gather_call(): pl.pallas_call(gather_kernel, out_shape=shape((X_LO * Z, V, V), BF16), in...  27 us
    unnamed x22, local copies, waits for them, and re-layouts  5.41 us
    pallas_call x1, Pallas kernels, backward_call(): pl.pallas_call(backward_kernel, out_shape=(shape((X_LO * Z, V, V), BF16),...  2.19 us

profile of v2, /device:TPU:1, one launch (start us, length us, event | category | flops | bytes accessed | tf_op | source)
XLA Modules:
  0.0 107.9 jit_solution(1260836762570586208)
XLA Ops:
  1.3 0.0 copy-start.4
  1.3 0.7 copy-done.4
  2.0 0.0 copy-start.5
  2.0 0.7 copy-done.5
  2.7 27.0 %gather_rows.1 = bf16[24,128,128]{2,1,0:T(8,128)(2,1)S(1)} custom-call(bf16[128,128]{1,0:T(8,128)(2,1)S(1)} %copy-done.4, bf16[1,128]{1,0:T(2,128)(2,1)S(1)} %bitcast.15), custom_call_target="tpu_custom_call" | custom-call | tf_op jit(solution)/shard_map/gather_rows/pallas_call | solution.py:448
  29.7 0.0 copy-start
  29.7 1.4 %copy-done = s32[1,1,48,32,256]{4,3,2,1,0:T(8,128)S(1)} copy-done((s32[1,1,48,32,256]{4,3,2,1,0:T(8,128)S(1)}, s32[1,1,48,32,256]{4,3,2,1,0:T(8,128)}, u32[]{:S(2)}) %copy-start) | copy-done | bytes 1572888
  31.1 0.0 copy-start.7
  31.1 0.7 copy-done.7
  31.8 0.0 copy-start.8
  31.8 0.7 copy-done.8
  32.4 0.0 copy-start.2
  32.4 0.0 copy-start.3
  32.4 0.0 copy-start.6
  32.4 0.0 copy-start.1
  32.4 0.0 copy-start.9
  32.4 1.7 %forward_tiles.1.partial = bf16[2,8,2,128,128]{4,3,2,1,0:T(8,128)(2,1)S(1)} custom-call(s32[48]{0:T(128)S(1)} %bitcast.18, s32[48]{0:T(128)S(1)} %bitcast.20, s32[1]{0:T(128)} %bitcast.9.count, bf16[12,256,128]{2,1,0:T(8,128)(2,1)S(1)} %bitcast.13, s32[48,32,256]{2,1,0:T(8,128)S(1)} %bitcast.11), custom_call_target="tpu_custom_call" | custom-call | tf_op jit(solution)/shard_map/forward_tiles/pallas_call | solution.py:460
  34.2 0.0 copy-done.2
  34.2 0.0 copy-done.3
  34.2 0.0 copy-done.6
  34.2 40.0 %vertex_part.1 = (bf16[128,256]{1,0:T(8,128)(2,1)S(1)}, bf16[2,8,2,128,128]{4,3,2,1,0:T(8,128)(2,1)S(1)}, f32[8,128]{1,0:T(8,128)S(1)}) custom-call(bf16[2,8,2,128,128]{4,3,2,1,0:T(8,128)(2,1)S(1)} %forward_tiles.1.partial, bf16[1,128]{1,0:T(2,128)(2,1)S(1)} %bitcast.16, bf16[128,256]{1,0:T(8,128)(2,1)S(1)} %copy-done.2, bf16[128,256]{1,0:T(8,128)(2,1)S(1)} %copy-done.3), custom_call_target="tpu_custom_call" | custom-call | tf_op jit(solution)/shard_map/vertex_part/pallas_call | solution.py:472
  74.2 0.0 copy-done.1
  74.2 0.0 copy-done.9
  74.3 2.2 %backward_tiles.1 = (bf16[24,128,128]{2,1,0:T(8,128)(2,1)S(1)}, bf16[128,256]{1,0:T(8,128)(2,1)}) custom-call(s32[48]{0:T(128)S(1)} %bitcast.19, s32[48]{0:T(128)S(1)} %bitcast.21, s32[1]{0:T(128)} %bitcast.10.count, bf16[2,8,2,128,128]{4,3,2,1,0:T(8,128)(2,1)S(1)} %get-tuple-element.10.source, s32[48,32,256]{2,1,0:T(8,128)S(1)} %bitcast.12, ...), custom_call_target="tpu_custom_call" | custom-call | tf_op jit(solution)/shard_map/backward_tiles/pallas_call | solution.py:496
  76.4 30.2 %scatter_rows.1 = (bf16[128,128]{1,0:T(8,128)(2,1)S(1)}, f32[2,8,2,8,128]{4,3,2,1,0:T(8,128)S(1)}) custom-call(bf16[24,128,128]{2,1,0:T(8,128)(2,1)S(1)} %get-tuple-element.13.partial, bf16[1,128]{1,0:T(2,128)(2,1)S(1)} %bitcast.17, f32[8,128]{1,0:T(8,128)S(1)} %get-tuple-element.14.piece), custom_call_target="tpu_custom_call" | custom-call | tf_op jit(solution)/shard_map/scatter_rows/pallas_call | solution.py:508
  106.7 0.6 copy.14
  107.3 0.7 copy.15
Async XLA Ops:
  1.3 0.8 copy-start.4
  2.0 0.7 copy-start.5
  29.7 1.4 %copy-start = (s32[1,1,48,32,256]{4,3,2,1,0:T(8,128)S(1)}, s32[1,1,48,32,256]{4,3,2,1,0:T(8,128)}, u32[]{:S(2)}) copy-start(s32[1,1,48,32,256]{4,3,2,1,0:T(8,128)} %param.15) | copy-start | bytes 4718596
  31.1 0.7 copy-start.7
  31.8 0.7 copy-start.8
  32.4 1.7 %copy-start.2 = (bf16[128,256]{1,0:T(8,128)(2,1)S(1)}, bf16[128,256]{1,0:T(8,128)(2,1)}, u32[]{:S(2)}) copy-start(bf16[128,256]{1,0:T(8,128)(2,1)} %weight.1) | copy-start | bytes 196612
  32.4 1.7 %copy-start.3 = (bf16[128,256]{1,0:T(8,128)(2,1)S(1)}, bf16[128,256]{1,0:T(8,128)(2,1)}, u32[]{:S(2)}) copy-start(bf16[128,256]{1,0:T(8,128)(2,1)} %cotangent.1) | copy-start | bytes 196612
  32.4 1.7 %copy-start.6 = (bf16[128]{0:T(256)(128)(2,1)S(1)}, bf16[128]{0:T(256)(128)(2,1)}, u32[]{:S(2)}) copy-start(bf16[128]{0:T(256)(128)(2,1)} %param.9) | copy-start | bytes 772
  32.4 41.8 %copy-start.1 = (s32[1,1,48,32,256]{4,3,2,1,0:T(8,128)S(1)}, s32[1,1,48,32,256]{4,3,2,1,0:T(8,128)}, u32[]{:S(2)}) copy-start(s32[1,1,48,32,256]{4,3,2,1,0:T(8,128)} %param.15) | copy-start | bytes 4718596
  32.4 41.8 %copy-start.9 = (s32[1,1,48]{2,1,0:T(1,128)S(1)}, s32[1,1,48]{2,1,0:T(1,128)}, u32[]{:S(2)}) copy-start(s32[1,1,48]{2,1,0:T(1,128)} %param.13) | copy-start | bytes 580

commit v3 on v2

v3 whole, which is shorter than its diff:
```python
import functools
import math

import jax
import jax.numpy as jnp
from jax import lax
from jax.experimental import pallas as pl
from jax.experimental.pallas import tpu as pltpu
from jax.sharding import PartitionSpec as P

MESH = pl.DeviceIdType.MESH
F32, BF16 = jnp.float32, jnp.bfloat16
X_LO, Z = 2, 12
X_HI, Y, CORES = 2, 8, 2
V = 128
VMEM_BYTES = 24 * 1024 * 1024
WHOLE = pl.BlockSpec(memory_space=pltpu.VMEM)
SCALARS = pl.BlockSpec(memory_space=pltpu.SMEM)


class Place:
    def __init__(self):
        row, col = lax.axis_index("row"), lax.axis_index("col")
        self.row, self.col = row, col
        self.x_lo, self.z = row // Z, row % Z
        self.x_hi, self.y, self.core = col // (Y * CORES), (col // CORES) % Y, col % CORES

    def at(self, x_lo=None, z=None, x_hi=None, y=None, core=None):
        x_lo = self.x_lo if x_lo is None else x_lo
        z = self.z if z is None else z
        x_hi = self.x_hi if x_hi is None else x_hi
        y = self.y if y is None else y
        core = self.core if core is None else core
        return (x_lo * Z + z, (x_hi * Y + y) * CORES + core)


def greet(peers):
    barrier = pltpu.get_barrier_semaphore()
    for peer in peers:
        pl.semaphore_signal(barrier, inc=1, device_id=peer, device_id_type=MESH)
    return lambda: pl.semaphore_wait(barrier, len(peers))


class Wire:
    def __init__(self, send, recv):
        self.send, self.recv, self.used, self.sent = send, recv, 0, []

    def slot(self):
        self.used += 1
        return self.used - 1

    def copy(self, slot, src, dst, to):
        return pltpu.make_async_remote_copy(
            src_ref=src, dst_ref=dst, send_sem=self.send.at[slot], recv_sem=self.recv.at[slot],
            device_id=to, device_id_type=MESH)

    def start(self, slot, src, dst, to):
        copy = self.copy(slot, src, dst, to)
        copy.start()
        self.sent.append(copy)

    def arrived(self, slot, dst, to):
        self.copy(slot, dst, dst, to).wait_recv()

    def finish(self):
        for copy in self.sent:
            copy.wait_send()


def row_gather(wire, me, out):
    def block(offset, pair=me.x_lo):
        return out.at[pair * Z + (me.z + offset) % Z]

    def to(offset):
        return me.at(z=(me.z + offset) % Z)

    partner, other = me.at(x_lo=1 - me.x_lo), 1 - me.x_lo
    near = {o: wire.slot() for o in (3, 9, 2, 10, 1, 11)}
    far = {o: wire.slot() for o in (3, 9, 2, 10, 1, 11)}
    cross = {o: wire.slot() for o in (0, 9, 3, 10, 2, 7, 5, 6)}
    side = {o: wire.slot() for o in (1, 11)}
    side_far = {o: wire.slot() for o in (1, 11)}

    def hand_over(offset):
        wire.start(cross[offset], block(offset), block(offset), partner)

    for o in near:
        wire.start(near[o], block(0), block(0), to(o))
    hand_over(0)
    yield
    wire.arrived(cross[0], block(0, other), partner)
    for o in side:
        wire.start(side[o], block(0, other), block(0, other), to(o))
    for o in near:
        source = Z - o
        wire.arrived(near[o], block(source), to(o))
        if o in (3, 9):
            sign = 1 if o == 3 else -1
            half = block(source).at[pl.ds(0 if o == 3 else V // 2, V // 2)]
            wire.start(far[o], half, half, to(3 * sign % Z))
            wire.start(far[2 * sign % Z], block(source), block(source), to(2 * sign % Z))
            wire.start(far[sign % Z], block(source), block(source), to(sign % Z))
        if o not in side:
            hand_over(source)
    yield
    for o, source in ((1, 9), (11, 3)):
        wire.arrived(cross[source], block(source, other), partner)
        wire.start(side_far[o], block(source, other), block(source, other), to(o))
    for o, source in ((2, 7), (10, 5)):
        wire.arrived(far[o], block(source), to(o))
        hand_over(source)
    wire.arrived(far[3], block(6).at[pl.ds(0, V // 2)], to(3))
    wire.arrived(far[9], block(6).at[pl.ds(V // 2, V // 2)], to(9))
    hand_over(6)
    yield
    for o, source in ((1, 8), (11, 4)):
        wire.arrived(far[o], block(source), to(o))
        wire.arrived(side[o], block(Z - o, other), to(o))
        wire.arrived(side_far[o], block(source, other), to(o))
    for o in (10, 2, 7, 5, 6):
        wire.arrived(cross[o], block(o, other), partner)


def row_reduce(wire, me, partial, cross_buf, ready, relay, final, done):
    def to(offset):
        return me.at(z=(me.z + offset) % Z)

    def term(pair, offset):
        return partial.at[pair * Z + (me.z + offset) % Z]

    partner, other = me.at(x_lo=1 - me.x_lo), 1 - me.x_lo
    order = (4, 8, 5, 7, 6, 3, 9, 2, 10)
    cross = {o: wire.slot() for o in order + (0,)}
    direct = {o: wire.slot() for o in (2, 10, 1, 11, 3, 9)}
    side = {o: wire.slot() for o in (1, 11)}
    relay_at = {1: 0, 11: 1, 2: 2, 10: 3, 3: 4, 9: 5}
    side_at = {1: 6, 11: 7}
    for o in order:
        wire.start(cross[o], term(other, o), cross_buf.at[(me.z + o) % Z], partner)
    for o in (1, 11):
        wire.start(side[o], term(other, o), relay.at[side_at[o]], to(o))
        wire.start(direct[o], term(me.x_lo, o), final.at[relay_at[o]], to(o))

    def value(offset):
        t = (me.z + offset) % Z
        wire.arrived(cross[offset], cross_buf.at[t], partner)
        return term(me.x_lo, offset)[...].astype(F32) + cross_buf[t].astype(F32)

    yield
    relayed = {o: wire.slot() for o in (1, 11, 2, 10, 3, 9)}
    low, high = pl.ds(0, V // 2), pl.ds(V // 2, V // 2)
    for o, hop in ((4, 1), (8, 11), (5, 2), (7, 10)):
        ready[o] = value(o).astype(BF16)
        wire.start(relayed[hop], ready.at[o], relay.at[relay_at[hop]], to(hop))
    ready[6] = value(6).astype(BF16)
    for hop, half in ((3, low), (9, high)):
        wire.start(relayed[hop], ready.at[6, half], relay.at[relay_at[hop], half], to(hop))
    total = term(other, 0)[...].astype(F32)
    for o in (1, 11):
        wire.arrived(side[o], relay.at[side_at[o]], to(o))
        total = total + relay[side_at[o]].astype(F32)
    ready[0] = total.astype(BF16)
    wire.start(cross[0], ready.at[0], cross_buf.at[me.z], partner)
    yield
    sums = {o: value(o) for o in (3, 9)}
    for o in (2, 10):
        ready[o] = value(o).astype(BF16)
        wire.start(direct[o], ready.at[o], final.at[relay_at[o]], to(o))
    yield
    for o, hops, half in ((3, (1, 2, 3), low), (9, (11, 10, 9), high)):
        total = sums[o]
        for hop in hops[:2]:
            wire.arrived(relayed[hop], relay.at[relay_at[hop]], to(hop))
            total = total + relay[relay_at[hop]].astype(F32)
        last = relay.at[relay_at[hops[2]], half]
        wire.arrived(relayed[hops[2]], last, to(hops[2]))
        cut = V // 2
        top, bottom = total[:cut], total[cut:]
        if o == 3:
            top = top + last[...].astype(F32)
        else:
            bottom = bottom + last[...].astype(F32)
        ready[o, low] = top.astype(BF16)
        ready[o, high] = bottom.astype(BF16)
        wire.start(direct[o], ready.at[o], final.at[relay_at[o]], to(o))
    yield
    total = value(0)
    for o in (1, 11, 2, 10, 3, 9):
        wire.arrived(direct[o], final.at[relay_at[o]], to(o))
        total = total + final[relay_at[o]].astype(F32)
    done(total)


def col_reduce(wire, me, partial, core_buf, cross_out, cross_buf, ready, final, done):
    sibling, partner = me.at(core=1 - me.core), me.at(x_hi=1 - me.x_hi)
    order = (4, 5, 3, 7, 1, 6, 2, 0)
    early = (4, 5, 3, 6, 2)
    cores = {o: wire.slot() for o in order}
    cross = {o: wire.slot() for o in early + (0,)}
    direct = {o: wire.slot() for o in order[:-1]}
    side = {o: wire.slot() for o in (1, 7)}
    side_at = {1: Y, 7: Y + 1}
    spot = lambda o: (me.y + o) % Y
    to = lambda o: me.at(y=spot(o))

    def pair_sum(o, x_hi):
        return partial[me.core, spot(o), x_hi].astype(F32) + core_buf[spot(o), x_hi].astype(F32)

    for o in order:
        wire.start(cores[o], partial.at[1 - me.core, spot(o)], core_buf.at[spot(o)], sibling)
    for o in order:
        wire.arrived(cores[o], core_buf.at[spot(o)], sibling)
        if o:
            cross_out[o] = pair_sum(o, 1 - me.x_hi).astype(BF16)
        if o in early:
            wire.start(cross[o], cross_out.at[o], cross_buf.at[spot(o)], partner)
        elif o:
            wire.start(side[o], cross_out.at[o], final.at[side_at[o]], to(o))
            ready[o] = pair_sum(o, me.x_hi).astype(BF16)
            wire.start(direct[o], ready.at[o], final.at[o], to(o))

    def value(o):
        wire.arrived(cross[o], cross_buf.at[spot(o)], partner)
        return pair_sum(o, me.x_hi) + cross_buf[spot(o)].astype(F32)

    for o in early:
        ready[o] = value(o).astype(BF16)
        wire.start(direct[o], ready.at[o], final.at[o], to(o))
        if o == 3:
            total = pair_sum(0, 1 - me.x_hi)
            for near in (1, 7):
                wire.arrived(side[near], final.at[side_at[near]], to(near))
                total = total + final[side_at[near]].astype(F32)
            cross_out[0] = total.astype(BF16)
            wire.start(cross[0], cross_out.at[0], cross_buf.at[me.y], partner)
    total = value(0)
    for o in (7, 1, 4, 5, 3, 6, 2):
        wire.arrived(direct[o], final.at[o], to(o))
        total = total + final[o].astype(F32)
    done(total)


def col_gather(wire, me, row_block):
    sibling, partner = me.at(core=1 - me.core), me.at(x_hi=1 - me.x_hi)

    def block(offset, x_hi, core=me.core):
        return row_block.at[core, (me.y + offset) % Y, x_hi]

    direct = {o: wire.slot() for o in range(1, Y)}
    cross = {o: wire.slot() for o in (0, 5, 3, 6, 2, 4)}
    side = {o: wire.slot() for o in (1, 7)}
    mine = {o: wire.slot() for o in range(Y)}
    theirs = {o: wire.slot() for o in range(Y)}
    own, other = block(0, me.x_hi), 1 - me.x_hi
    to = lambda o: me.at(y=(me.y + o) % Y)

    def hand_over(o):
        here = block(o, me.x_hi)
        if o in cross:
            wire.start(cross[o], here, here, partner)
        wire.start(mine[o], here, here, sibling)

    def pass_on(slot, o, sender):
        here = block(o, other)
        wire.arrived(slot, here, sender)
        wire.start(theirs[o], here, here, sibling)

    for o in (4, 3, 5, 2, 6, 1, 7):
        wire.start(direct[o], own, own, to(o))
    hand_over(0)
    yield
    wire.arrived(cross[0], block(0, other), partner)
    for o in side:
        wire.start(side[o], block(0, other), block(0, other), to(o))
    wire.start(theirs[0], block(0, other), block(0, other), sibling)
    for o in (3, 5, 2, 6):
        wire.arrived(direct[o], block(Y - o, me.x_hi), to(o))
        hand_over(Y - o)
    yield
    for o in (4, 1, 7):
        wire.arrived(direct[o], block(Y - o, me.x_hi), to(o))
        hand_over(Y - o)
    yield
    for o in (5, 3):
        pass_on(cross[o], o, partner)
    for o in side:
        pass_on(side[o], Y - o, to(o))
    yield
    for o in (6, 2, 4):
        pass_on(cross[o], o, partner)
    yield
    for o in range(Y):
        wire.arrived(mine[o], block(o, me.x_hi, 1 - me.core), sibling)
        wire.arrived(theirs[o], block(o, other, 1 - me.core), sibling)


def together(*jobs):
    jobs = list(jobs)
    while jobs:
        for job in list(jobs):
            try:
                next(job)
            except StopIteration:
                jobs.remove(job)


def in_turn(first, second, order):
    for letter in order:
        next(first if letter == "A" else second, None)
    together(first, second)


def column_of(row_vector):
    return jnp.transpose(jnp.broadcast_to(row_vector, (V, V)))


def unpack(words):
    parts = []
    for half in (0, 1):
        part = words[16 * half:16 * half + 16]
        for k in range(8):
            parts.append(jnp.bitwise_and(jnp.right_shift(part, k), 1).astype(F32).astype(BF16))
    return jnp.concatenate(parts, axis=0)


def gather_kernel(count, features, scale, bits, out, masks, send, recv):
    me = Place()
    peers = [me.at(z=(me.z + d) % Z) for d in (1, 2, 3, 9, 10, 11)]
    ready = greet(peers + [me.at(x_lo=1 - me.x_lo)])
    scaled = features[...].astype(F32) * column_of(scale[...].astype(F32))
    out[me.row] = scaled.astype(BF16)
    ready()
    wire = Wire(send, recv)
    gathering = row_gather(wire, me, out)
    next(gathering)
    live = count[0]

    def turn(t, _):
        masks[t] = unpack(jnp.where(t < live, bits[t], 0))
        return 0

    lax.fori_loop(0, bits.shape[0], turn, 0)
    together(gathering)
    wire.finish()


UNROLL = 4


def live_tiles(count, body):
    def turn(step, _):
        for u in range(UNROLL):
            body(step * UNROLL + u)
        return 0

    lax.fori_loop(0, (count[0] + UNROLL - 1) // UNROLL, turn, 0)


def forward_kernel(rows, cols, count, source, masks, out, acc):
    acc[...] = jnp.zeros_like(acc)

    def body(slot):
        i = rows[slot]
        acc[i] = acc[i] + jnp.dot(masks[slot], source[cols[slot]], preferred_element_type=F32)

    live_tiles(count, body)
    for i in range(acc.shape[0]):
        for half in (0, 1):
            out[half, i % Y, i // Y] = acc[i, half * V:half * V + V, :].astype(BF16)


def backward_kernel(rows, cols, count, source, masks, act_in, out, act_out, acc):
    acc[...] = jnp.zeros_like(acc)
    act_out[...] = act_in[...]

    def body(slot):
        i, j = rows[slot], cols[slot]
        y, x_hi = i % Y, i // Y
        back = jnp.concatenate([source[0, y, x_hi], source[1, y, x_hi]], axis=1)
        acc[j] = acc[j] + jnp.dot(back, masks[slot], preferred_element_type=F32)

    live_tiles(count, body)
    for j in range(acc.shape[0]):
        for half in (0, 1):
            out[2 * j + half] = acc[j, :, half * V:half * V + V].astype(BF16)


def vertex_kernel(partial, scale, weight, cotangent, act, row_block, piece,
                  core_buf, cross_out, cross_buf, outgoing, final, natural, grad, grad_core, grad_mine,
                  grad_y, grad_x, send, recv):
    me = Place()
    partner, sibling = me.at(x_hi=1 - me.x_hi), me.at(core=1 - me.core)
    y_peers = [me.at(y=(me.y + d) % Y) for d in range(1, Y)]
    x_ring = {(lo, hi): me.at(x_lo=(me.x_lo + lo) % X_LO, x_hi=(me.x_hi + hi) % X_HI)
              for lo, hi in ((0, 1), (1, 0), (1, 1))}
    ready = greet([sibling] + y_peers + list(x_ring.values()))
    wire = Wire(send, recv)
    scale_row = scale[...].astype(F32)
    scale_col = column_of(scale_row)
    ready()
    pieces = []
    col_reduce(wire, me, partial, core_buf, cross_out, cross_buf, outgoing, final, pieces.append)
    summed = pieces[0]
    for k in range(8):
        natural[pl.ds(k, 16, stride=8), :] = summed[16 * k:16 * k + 16]
    hidden = (natural[...] * scale_col).astype(BF16)
    pre_act = jnp.dot(hidden, weight[...], preferred_element_type=F32)
    sigmoid = 1.0 / (1.0 + jnp.exp(-pre_act))
    slope = sigmoid * (1.0 + pre_act * (1.0 - sigmoid))
    slope_term = (cotangent[...].astype(F32) * slope).astype(BF16)
    back = lax.dot_general(weight[...], slope_term, (((1,), (1,)), ((), ())),
                           preferred_element_type=F32)
    back = (back * scale_row).astype(BF16)
    from_v = lax.broadcasted_iota(jnp.int32, (V, V), 0)
    to_v = lax.broadcasted_iota(jnp.int32, (V, V), 1)
    swap = (from_v == 8 * (to_v % 16) + to_v // 16).astype(F32).astype(BF16)
    row_block[me.core, me.y, me.x_hi] = jnp.dot(
        back, swap, preferred_element_type=F32).astype(BF16)

    def weight_part():
        act[...] = (pre_act * sigmoid).astype(BF16)
        grad[...] = lax.dot_general(hidden, slope_term, (((0,), (0,)), ((), ())),
                                    preferred_element_type=F32).reshape(2, V // 2, 2 * V)
        slot = wire.slot()
        wire.start(slot, grad.at[1 - me.core], grad_core, sibling)
        yield
        wire.arrived(slot, grad_core, sibling)
        grad_mine[...] = (grad[me.core] + grad_core[...]).reshape(Y, V // 16, 2 * V)
        slots = [wire.slot() for _ in y_peers]
        for d, peer in enumerate(y_peers, 1):
            wire.start(slots[d - 1], grad_mine.at[(me.y + d) % Y], grad_y.at[me.y], peer)
        grad_y[me.y] = grad_mine[me.y]
        yield
        for d, peer in enumerate(y_peers, 1):
            wire.arrived(slots[d - 1], grad_y.at[(me.y + Y - d) % Y], peer)
        total = grad_y[0]
        for k in range(1, Y):
            total = total + grad_y[k]
        place = lambda lo, hi: grad_x.at[((me.x_lo + lo) % X_LO) * X_HI + (me.x_hi + hi) % X_HI]
        place(0, 0)[...] = total
        slots = {shift: wire.slot() for shift in x_ring}
        for shift in x_ring:
            wire.start(slots[shift], place(0, 0), place(0, 0), x_ring[shift])
        yield
        for shift in x_ring:
            wire.arrived(slots[shift], place(*shift), x_ring[shift])
        total = grad_x[0]
        for k in range(1, X_LO * X_HI):
            total = total + grad_x[k]
        piece[...] = total

    in_turn(col_gather(wire, me, row_block), weight_part(), "ABBABAB")
    wire.finish()


def scatter_kernel(partial, scale, piece, grad_in, weight_grad, cross_buf, outgoing, relay, final,
                   sums, send, recv):
    me = Place()
    partner, sibling = me.at(x_lo=1 - me.x_lo), me.at(core=1 - me.core)
    z_near = {o: me.at(z=(me.z + o) % Z) for o in (1, 2, 3, 9, 10, 11)}
    y_peers = [me.at(y=(me.y + d) % Y) for d in range(1, Y)]
    ready = greet([partner, sibling] + y_peers + list(z_near.values()))
    wire = Wire(send, recv)
    scale_row = scale[...].astype(F32)
    ready()

    def done(total):
        grad_in[...] = jnp.transpose(total * scale_row).astype(BF16)

    def weight_part():
        at = lambda offset: sums.at[(me.z + offset) % Z]
        near = {o: wire.slot() for o in (3, 9, 2, 10, 1, 11)}
        far = {o: wire.slot() for o in (3, 2, 10, 1, 11)}
        at(0)[...] = piece[...]
        for o in near:
            wire.start(near[o], at(0), at(0), z_near[o])
        yield
        for o in near:
            wire.arrived(near[o], at(Z - o), z_near[o])
            if o in (3, 9):
                for hop in ((3, 2, 1) if o == 3 else (10, 11)):
                    wire.start(far[hop], at(Z - o), at(Z - o), z_near[hop])
        yield
        for o, source in ((1, 8), (11, 4), (2, 7), (10, 5), (3, 6)):
            wire.arrived(far[o], at(source), z_near[o])
        total = sums[0]
        for k in range(1, Z):
            total = total + sums[k]
        spot = weight_grad.at[me.core, me.y]
        spot[...] = total / math.sqrt(X_LO * Z * X_HI * Y * CORES * V)
        slots = [wire.slot() for _ in y_peers]
        for d, peer in enumerate(y_peers, 1):
            wire.start(slots[d - 1], spot, spot, peer)
        yield
        for d, peer in enumerate(y_peers, 1):
            wire.arrived(slots[d - 1], weight_grad.at[me.core, (me.y + Y - d) % Y], peer)
        slot = wire.slot()
        wire.start(slot, weight_grad.at[me.core], weight_grad.at[me.core], sibling)
        yield
        wire.arrived(slot, weight_grad.at[1 - me.core], sibling)

    in_turn(row_reduce(wire, me, partial, cross_buf, outgoing, relay, final, done), weight_part(),
            "ABABABABA")
    wire.finish()


def sems(count):
    return [pltpu.SemaphoreType.DMA((count,)), pltpu.SemaphoreType.DMA((count,))]


def shape(extent, dtype):
    return jax.ShapeDtypeStruct(extent, dtype)


def talking(collective_id):
    return pltpu.CompilerParams(
        collective_id=collective_id, has_side_effects=True, vmem_limit_bytes=VMEM_BYTES)


def gather_call(count, features, scale, bits):
    return pl.pallas_call(
        gather_kernel,
        out_shape=(shape((X_LO * Z, V, V), BF16), shape((bits.shape[0], 2 * V, 2 * V), BF16)),
        in_specs=[SCALARS] + [WHOLE] * 3,
        out_specs=(WHOLE,) * 2,
        scratch_shapes=sems(24),
        compiler_params=talking(0),
        name="gather_rows",
    )(count, features, scale, bits)


def forward_call(rows, cols, count, source, masks):
    return pl.pallas_call(
        forward_kernel,
        out_shape=shape((CORES, Y, X_HI, V, V), BF16),
        in_specs=[SCALARS] * 3 + [WHOLE] * 2,
        out_specs=WHOLE,
        scratch_shapes=[pltpu.VMEM((X_HI * Y, 2 * V, V), F32)],
        compiler_params=pltpu.CompilerParams(vmem_limit_bytes=VMEM_BYTES),
        name="forward_tiles",
    )(rows, cols, count, source, masks)


def vertex_call(partial, scale, weight, cotangent):
    return pl.pallas_call(
        vertex_kernel,
        out_shape=(shape((V, 2 * V), BF16), shape((CORES, Y, X_HI, V, V), BF16), shape((8, 2 * V), F32)),
        in_specs=[WHOLE] * 4,
        out_specs=(WHOLE,) * 3,
        scratch_shapes=[
            pltpu.VMEM((Y, X_HI, V, V), BF16),
            pltpu.VMEM((Y, V, V), BF16),
            pltpu.VMEM((Y, V, V), BF16),
            pltpu.VMEM((Y, V, V), BF16),
            pltpu.VMEM((Y + 2, V, V), BF16),
            pltpu.VMEM((V, V), F32),
            pltpu.VMEM((2, V // 2, 2 * V), F32),
            pltpu.VMEM((V // 2, 2 * V), F32),
            pltpu.VMEM((Y, 8, 2 * V), F32),
            pltpu.VMEM((Y, 8, 2 * V), F32),
            pltpu.VMEM((X_LO * X_HI, 8, 2 * V), F32),
        ] + sems(72),
        compiler_params=talking(1),
        name="vertex_part",
    )(partial, scale, weight, cotangent)


def backward_call(rows, cols, count, source, masks, act):
    return pl.pallas_call(
        backward_kernel,
        out_shape=(shape((X_LO * Z, V, V), BF16), shape(act.shape, act.dtype)),
        in_specs=[SCALARS] * 3 + [WHOLE] * 3,
        out_specs=(WHOLE,) * 2,
        scratch_shapes=[pltpu.VMEM((X_LO * Z // 2, V, 2 * V), F32)],
        compiler_params=pltpu.CompilerParams(vmem_limit_bytes=VMEM_BYTES),
        name="backward_tiles",
    )(rows, cols, count, source, masks, act)


def scatter_call(partial, scale, piece):
    return pl.pallas_call(
        scatter_kernel,
        out_shape=(shape((V, V), BF16), shape((CORES, Y, 8, 2 * V), F32)),
        in_specs=[WHOLE] * 3,
        out_specs=(WHOLE,) * 2,
        scratch_shapes=[
            pltpu.VMEM((Z, V, V), BF16),
            pltpu.VMEM((Z, V, V), BF16),
            pltpu.VMEM((8, V, V), BF16),
            pltpu.VMEM((6, V, V), BF16),
            pltpu.VMEM((Z, 8, 2 * V), F32),
        ] + sems(48),
        compiler_params=talking(2),
        name="scatter_rows",
    )(partial, scale, piece)


def on_device(features, deg_scale, weight, cotangent, tile_rows, tile_cols, tile_count, tile_bits):
    rows, cols, count, bits = tile_rows[0, 0], tile_cols[0, 0], tile_count[0], tile_bits[0, 0]
    scale = deg_scale.reshape(1, V)
    column_block, masks = gather_call(count, features, scale, bits)
    partial = forward_call(rows, cols, count, column_block.reshape(Z, 2 * V, V), masks)
    act, row_block, piece = vertex_call(partial, scale, weight, cotangent)
    partial_back, activations = backward_call(rows, cols, count, row_block, masks, act)
    input_grad, grad = scatter_call(partial_back, scale, piece)
    weight_grad = grad.reshape(V, 2 * V)
    return (activations, input_grad, weight_grad)


def solution(mesh):
    in_specs = (
        P(("row", "col"), None),
        P(("row", "col")),
        P(),
        P(("row", "col"), None),
        P("row", "col", None),
        P("row", "col", None),
        P("row", "col"),
        P("row", "col", None, None, None),
    )
    out_specs = (P(("row", "col"), None), P(("row", "col"), None), P())
    return jax.shard_map(
        on_device, mesh=mesh, in_specs=in_specs, out_specs=out_specs, check_vma=False)
```

time: 108 us -> 102 us (0.944)
  Pallas kernels: 101 us -> 94.9 us
    pallas_call x1, Pallas kernels: 30.2 us -> 23.5 us  [scatter_call(): pl.pallas_call(scatter_kernel, out_shape=(shape((V, V), BF16), shape((COR...]
    pallas_call x1, Pallas kernels: 40 us -> 41.3 us  [vertex_call(): pl.pallas_call(vertex_kernel, out_shape=(shape((V, 2 * V), BF16), shape((...]
where the time goes in v3:
time: 102 us
  Pallas kernels  94.9 us (93%)
  local copies, waits for them, and re-layouts  5.41 us (5%)
  between operations  1.42 us (1%)
    pallas_call x1, Pallas kernels, vertex_call(): pl.pallas_call(vertex_kernel, out_shape=(shape((V, 2 * V), BF16), shape((...  41.3 us
    pallas_call x1, Pallas kernels, gather_call(): pl.pallas_call(gather_kernel, out_shape=(shape((X_LO * Z, V, V), BF16), s...  27 us
    pallas_call x1, Pallas kernels, scatter_call(): pl.pallas_call(scatter_kernel, out_shape=(shape((V, V), BF16), shape((COR...  23.5 us
    unnamed x22, local copies, waits for them, and re-layouts  5.41 us

profile of v3, /device:TPU:1, one launch (start us, length us, event | category | flops | bytes accessed | tf_op | source)
XLA Modules:
  0.0 101.7 jit_solution(11238298722502591000)
XLA Ops:
  0.6 0.0 copy-start.9
  0.6 0.0 copy-start.7
  0.7 0.0 copy-start.5
  1.3 0.0 copy-start
  1.3 1.4 %copy-done = s32[1,1,48,32,256]{4,3,2,1,0:T(8,128)S(1)} copy-done((s32[1,1,48,32,256]{4,3,2,1,0:T(8,128)S(1)}, s32[1,1,48,32,256]{4,3,2,1,0:T(8,128)}, u32[]{:S(2)}) %copy-start) | copy-done | bytes 1572888
  2.7 0.0 copy-start.3
  2.7 0.8 copy-done.3
  3.5 0.0 copy-start.4
  3.5 0.7 copy-done.4
  4.2 0.0 copy-start.1
  4.2 0.0 copy-start.2
  4.2 27.0 %gather_rows.1 = (bf16[24,128,128]{2,1,0:T(8,128)(2,1)S(1)}, bf16[48,256,256]{2,1,0:T(8,128)(2,1)S(1)}) custom-call(s32[1]{0:T(128)} %bitcast.7.count, bf16[128,128]{1,0:T(8,128)(2,1)S(1)} %copy-done.3, bf16[1,128]{1,0:T(2,128)(2,1)S(1)} %bitcast.13, s32[48,32,256]{2,1,0:T(8,128)S(1)} %bitcast.10), custom_call_target="tpu_custom_call" | custom-call | tf_op jit(solution)/shard_map/gather_rows/pallas_call | solution.py:521
  31.1 0.0 copy-start.6
  31.1 0.6 copy-done.6
  31.8 0.0 copy-start.8
  31.8 0.7 copy-done.8
  32.4 1.4 %forward_tiles.1.partial = bf16[2,8,2,128,128]{4,3,2,1,0:T(8,128)(2,1)S(1)} custom-call(s32[48]{0:T(128)S(1)} %bitcast.16, s32[48]{0:T(128)S(1)} %bitcast.18, s32[1]{0:T(128)} %bitcast.8.count, bf16[12,256,128]{2,1,0:T(8,128)(2,1)S(1)} %bitcast.11, bf16[48,256,256]{2,1,0:T(8,128)(2,1)S(1)} %get-tuple-element.13.masks), custom_call_target="tpu_custom_call" | custom-call | tf_op jit(solution)/shard_map/forward_tiles/pallas_call | solution.py:533
  33.8 0.0 copy-done.5
  33.8 0.0 copy-done.1
  33.8 0.0 copy-done.2
  33.9 41.3 %vertex_part.1 = (bf16[128,256]{1,0:T(8,128)(2,1)S(1)}, bf16[2,8,2,128,128]{4,3,2,1,0:T(8,128)(2,1)S(1)}, f32[8,256]{1,0:T(8,128)S(1)}) custom-call(bf16[2,8,2,128,128]{4,3,2,1,0:T(8,128)(2,1)S(1)} %forward_tiles.1.partial, bf16[1,128]{1,0:T(2,128)(2,1)S(1)} %bitcast.14, bf16[128,256]{1,0:T(8,128)(2,1)S(1)} %copy-done.1, bf16[128,256]{1,0:T(8,128)(2,1)S(1)} %copy-done.2), custom_call_target="tpu_custom_call" | custom-call | tf_op jit(solution)/shard_map/vertex_part/pallas_call | solution.py:545
  75.2 0.0 copy-done.9
  75.2 0.0 copy-done.7
  75.2 1.8 %backward_tiles.1 = (bf16[24,128,128]{2,1,0:T(8,128)(2,1)S(1)}, bf16[128,256]{1,0:T(8,128)(2,1)}) custom-call(s32[48]{0:T(128)S(1)} %bitcast.17, s32[48]{0:T(128)S(1)} %bitcast.19, s32[1]{0:T(128)} %bitcast.9.count, bf16[2,8,2,128,128]{4,3,2,1,0:T(8,128)(2,1)S(1)} %get-tuple-element.14.source, bf16[48,256,256]{2,1,0:T(8,128)(2,1)S(1)} %get-tuple-element.13.masks, ...), custom_call_target="tpu_custom_call" | custom-call | tf_op jit(solution)/shard_map/backward_tiles/pallas_call | solution.py:569
  77.0 23.5 %scatter_rows.1 = (bf16[128,128]{1,0:T(8,128)(2,1)S(1)}, f32[2,8,8,256]{3,2,1,0:T(8,128)S(1)}) custom-call(bf16[24,128,128]{2,1,0:T(8,128)(2,1)S(1)} %get-tuple-element.17.partial, bf16[1,128]{1,0:T(2,128)(2,1)S(1)} %bitcast.15, f32[8,256]{1,0:T(8,128)S(1)} %get-tuple-element.18.piece), custom_call_target="tpu_custom_call" | custom-call | tf_op jit(solution)/shard_map/scatter_rows/pallas_call | solution.py:581
  100.5 0.6 copy.14
  101.1 0.7 copy.15
Async XLA Ops:
  0.6 74.5 %copy-start.9 = (s32[1,1,48]{2,1,0:T(1,128)S(1)}, s32[1,1,48]{2,1,0:T(1,128)}, u32[]{:S(2)}) copy-start(s32[1,1,48]{2,1,0:T(1,128)} %param.13) | copy-start | bytes 580
  0.6 74.5 %copy-start.7 = (s32[1,1,48]{2,1,0:T(1,128)S(1)}, s32[1,1,48]{2,1,0:T(1,128)}, u32[]{:S(2)}) copy-start(s32[1,1,48]{2,1,0:T(1,128)} %param.12) | copy-start | bytes 580
  0.7 33.2 %copy-start.5 = (bf16[128]{0:T(256)(128)(2,1)S(1)}, bf16[128]{0:T(256)(128)(2,1)}, u32[]{:S(2)}) copy-start(bf16[128]{0:T(256)(128)(2,1)} %param.9) | copy-start | bytes 772
  1.3 1.4 %copy-start = (s32[1,1,48,32,256]{4,3,2,1,0:T(8,128)S(1)}, s32[1,1,48,32,256]{4,3,2,1,0:T(8,128)}, u32[]{:S(2)}) copy-start(s32[1,1,48,32,256]{4,3,2,1,0:T(8,128)} %param.15) | copy-start | bytes 4718596
  2.7 0.8 copy-start.3
  3.5 0.7 copy-start.4
  4.2 29.7 %copy-start.1 = (bf16[128,256]{1,0:T(8,128)(2,1)S(1)}, bf16[128,256]{1,0:T(8,128)(2,1)}, u32[]{:S(2)}) copy-start(bf16[128,256]{1,0:T(8,128)(2,1)} %weight.1) | copy-start | bytes 196612
  4.2 29.7 %copy-start.2 = (bf16[128,256]{1,0:T(8,128)(2,1)S(1)}, bf16[128,256]{1,0:T(8,128)(2,1)}, u32[]{:S(2)}) copy-start(bf16[128,256]{1,0:T(8,128)(2,1)} %cotangent.1) | copy-start | bytes 196612
  31.1 0.7 copy-start.6
  31.8 0.7 copy-start.8

commit v4 on v3

--- a/solution.py
+++ b/solution.py
@@ -149,9 +149,12 @@
     yield
     relayed = {o: wire.slot() for o in (1, 11, 2, 10, 3, 9)}
     low, high = pl.ds(0, V // 2), pl.ds(V // 2, V // 2)
-    for o, hop in ((4, 1), (8, 11), (5, 2), (7, 10)):
-        ready[o] = value(o).astype(BF16)
-        wire.start(relayed[hop], ready.at[o], relay.at[relay_at[hop]], to(hop))
+    for some in (((4, 1), (8, 11)), ((5, 2), (7, 10))):
+        for o, hop in some:
+            ready[o] = value(o).astype(BF16)
+            wire.start(relayed[hop], ready.at[o], relay.at[relay_at[hop]], to(hop))
+        if o == 8:
+            yield
     ready[6] = value(6).astype(BF16)
     for hop, half in ((3, low), (9, high)):
         wire.start(relayed[hop], ready.at[6, half], relay.at[relay_at[hop], half], to(hop))
@@ -347,10 +350,12 @@
 UNROLL = 4
 
 
-def live_tiles(count, body):
+def live_tiles(count, product, place, acc):
     def turn(step, _):
-        for u in range(UNROLL):
-            body(step * UNROLL + u)
+        slots = [step * UNROLL + u for u in range(UNROLL)]
+        products = [product(slot) for slot in slots]
+        for slot, value in zip(slots, products):
+            acc[place(slot)] = acc[place(slot)] + value
         return 0
 
     lax.fori_loop(0, (count[0] + UNROLL - 1) // UNROLL, turn, 0)
@@ -359,11 +364,10 @@
 def forward_kernel(rows, cols, count, source, masks, out, acc):
     acc[...] = jnp.zeros_like(acc)
 
-    def body(slot):
-        i = rows[slot]
-        acc[i] = acc[i] + jnp.dot(masks[slot], source[cols[slot]], preferred_element_type=F32)
-
-    live_tiles(count, body)
+    def product(slot):
+        return jnp.dot(masks[slot], source[cols[slot]], preferred_element_type=F32)
+
+    live_tiles(count, product, lambda slot: rows[slot], acc)
     for i in range(acc.shape[0]):
         for half in (0, 1):
             out[half, i % Y, i // Y] = acc[i, half * V:half * V + V, :].astype(BF16)
@@ -373,13 +377,13 @@
     acc[...] = jnp.zeros_like(acc)
     act_out[...] = act_in[...]
 
-    def body(slot):
-        i, j = rows[slot], cols[slot]
+    def product(slot):
+        i = rows[slot]
         y, x_hi = i % Y, i // Y
         back = jnp.concatenate([source[0, y, x_hi], source[1, y, x_hi]], axis=1)
-        acc[j] = acc[j] + jnp.dot(back, masks[slot], preferred_element_type=F32)
-
-    live_tiles(count, body)
+        return jnp.dot(back, masks[slot], preferred_element_type=F32)
+
+    live_tiles(count, product, lambda slot: cols[slot], acc)
     for j in range(acc.shape[0]):
         for half in (0, 1):
             out[2 * j + half] = acc[j, :, half * V:half * V + V].astype(BF16)
@@ -449,7 +453,7 @@
             total = total + grad_x[k]
         piece[...] = total
 
-    in_turn(col_gather(wire, me, row_block), weight_part(), "ABBABAB")
+    in_turn(col_gather(wire, me, row_block), weight_part(), "ABBABAAB")
     wire.finish()
 
 
@@ -500,7 +504,7 @@
         wire.arrived(slot, weight_grad.at[1 - me.core], sibling)
 
     in_turn(row_reduce(wire, me, partial, cross_buf, outgoing, relay, final, done), weight_part(),
-            "ABABABABA")
+            "ABABAABABA")
     wire.finish()
 
 

time: 102 us -> 102 us (level)
    pallas_call x1, Pallas kernels: 41.3 us -> 39.2 us  [vertex_call(): pl.pallas_call(vertex_kernel, out_shape=(shape((V, 2 * V), BF16), shape((...]
    pallas_call x1, Pallas kernels: 1.38 us -> 2.59 us  [forward_call(): pl.pallas_call(forward_kernel, out_shape=shape((CORES, Y, X_HI, V, V), BF...]
    pallas_call x1, Pallas kernels: 1.79 us -> 2.82 us  [backward_call(): pl.pallas_call(backward_kernel, out_shape=(shape((X_LO * Z, V, V), BF16),...]
where the time goes in v4:
time: 102 us
  Pallas kernels  95.3 us (93%)
  local copies, waits for them, and re-layouts  5.41 us (5%)
  between operations  1.42 us (1%)
    pallas_call x1, Pallas kernels, vertex_call(): pl.pallas_call(vertex_kernel, out_shape=(shape((V, 2 * V), BF16), shape((...  39.2 us
    pallas_call x1, Pallas kernels, gather_call(): pl.pallas_call(gather_kernel, out_shape=(shape((X_LO * Z, V, V), BF16), s...  27 us
    pallas_call x1, Pallas kernels, scatter_call(): pl.pallas_call(scatter_kernel, out_shape=(shape((V, V), BF16), shape((COR...  23.8 us
    unnamed x22, local copies, waits for them, and re-layouts  5.41 us
    pallas_call x1, Pallas kernels, backward_call(): pl.pallas_call(backward_kernel, out_shape=(shape((X_LO * Z, V, V), BF16),...  2.82 us
    pallas_call x1, Pallas kernels, forward_call(): pl.pallas_call(forward_kernel, out_shape=shape((CORES, Y, X_HI, V, V), BF...  2.59 us

profile of v4, /device:TPU:1, one launch (start us, length us, event | category | flops | bytes accessed | tf_op | source)
XLA Modules:
  0.0 102.1 jit_solution(6127868743011039775)
XLA Ops:
  0.6 0.0 copy-start.9
  0.6 0.0 copy-start.7
  0.7 0.0 copy-start.5
  1.3 0.0 copy-start
  1.3 1.4 %copy-done = s32[1,1,48,32,256]{4,3,2,1,0:T(8,128)S(1)} copy-done((s32[1,1,48,32,256]{4,3,2,1,0:T(8,128)S(1)}, s32[1,1,48,32,256]{4,3,2,1,0:T(8,128)}, u32[]{:S(2)}) %copy-start) | copy-done | bytes 1572888
  2.7 0.0 copy-start.3
  2.7 0.8 copy-done.3
  3.5 0.0 copy-start.4
  3.5 0.7 copy-done.4
  4.2 0.0 copy-start.1
  4.2 0.0 copy-start.2
  4.2 27.0 %gather_rows.1 = (bf16[24,128,128]{2,1,0:T(8,128)(2,1)S(1)}, bf16[48,256,256]{2,1,0:T(8,128)(2,1)S(1)}) custom-call(s32[1]{0:T(128)} %bitcast.7.count, bf16[128,128]{1,0:T(8,128)(2,1)S(1)} %copy-done.3, bf16[1,128]{1,0:T(2,128)(2,1)S(1)} %bitcast.13, s32[48,32,256]{2,1,0:T(8,128)S(1)} %bitcast.10), custom_call_target="tpu_custom_call" | custom-call | tf_op jit(solution)/shard_map/gather_rows/pallas_call | solution.py:525
  31.1 0.0 copy-start.6
  31.1 0.6 copy-done.6
  31.8 0.0 copy-start.8
  31.8 0.7 copy-done.8
  32.4 2.6 %forward_tiles.1.partial = bf16[2,8,2,128,128]{4,3,2,1,0:T(8,128)(2,1)S(1)} custom-call(s32[48]{0:T(128)S(1)} %bitcast.16, s32[48]{0:T(128)S(1)} %bitcast.18, s32[1]{0:T(128)} %bitcast.8.count, bf16[12,256,128]{2,1,0:T(8,128)(2,1)S(1)} %bitcast.11, bf16[48,256,256]{2,1,0:T(8,128)(2,1)S(1)} %get-tuple-element.13.masks), custom_call_target="tpu_custom_call" | custom-call | tf_op jit(solution)/shard_map/forward_tiles/pallas_call | solution.py:537
  35.0 0.0 copy-done.5
  35.0 0.0 copy-done.1
  35.1 0.0 copy-done.2
  35.1 39.2 %vertex_part.1 = (bf16[128,256]{1,0:T(8,128)(2,1)S(1)}, bf16[2,8,2,128,128]{4,3,2,1,0:T(8,128)(2,1)S(1)}, f32[8,256]{1,0:T(8,128)S(1)}) custom-call(bf16[2,8,2,128,128]{4,3,2,1,0:T(8,128)(2,1)S(1)} %forward_tiles.1.partial, bf16[1,128]{1,0:T(2,128)(2,1)S(1)} %bitcast.14, bf16[128,256]{1,0:T(8,128)(2,1)S(1)} %copy-done.1, bf16[128,256]{1,0:T(8,128)(2,1)S(1)} %copy-done.2), custom_call_target="tpu_custom_call" | custom-call | tf_op jit(solution)/shard_map/vertex_part/pallas_call | solution.py:549
  74.2 0.0 copy-done.9
  74.3 0.0 copy-done.7
  74.3 2.8 %backward_tiles.1 = (bf16[24,128,128]{2,1,0:T(8,128)(2,1)S(1)}, bf16[128,256]{1,0:T(8,128)(2,1)}) custom-call(s32[48]{0:T(128)S(1)} %bitcast.17, s32[48]{0:T(128)S(1)} %bitcast.19, s32[1]{0:T(128)} %bitcast.9.count, bf16[2,8,2,128,128]{4,3,2,1,0:T(8,128)(2,1)S(1)} %get-tuple-element.14.source, bf16[48,256,256]{2,1,0:T(8,128)(2,1)S(1)} %get-tuple-element.13.masks, ...), custom_call_target="tpu_custom_call" | custom-call | tf_op jit(solution)/shard_map/backward_tiles/pallas_call | solution.py:573
  77.1 23.8 %scatter_rows.1 = (bf16[128,128]{1,0:T(8,128)(2,1)S(1)}, f32[2,8,8,256]{3,2,1,0:T(8,128)S(1)}) custom-call(bf16[24,128,128]{2,1,0:T(8,128)(2,1)S(1)} %get-tuple-element.17.partial, bf16[1,128]{1,0:T(2,128)(2,1)S(1)} %bitcast.15, f32[8,256]{1,0:T(8,128)S(1)} %get-tuple-element.18.piece), custom_call_target="tpu_custom_call" | custom-call | tf_op jit(solution)/shard_map/scatter_rows/pallas_call | solution.py:585
  100.9 0.6 copy.14
  101.5 0.7 copy.15
Async XLA Ops:
  0.6 73.6 %copy-start.9 = (s32[1,1,48]{2,1,0:T(1,128)S(1)}, s32[1,1,48]{2,1,0:T(1,128)}, u32[]{:S(2)}) copy-start(s32[1,1,48]{2,1,0:T(1,128)} %param.13) | copy-start | bytes 580
  0.6 73.6 %copy-start.7 = (s32[1,1,48]{2,1,0:T(1,128)S(1)}, s32[1,1,48]{2,1,0:T(1,128)}, u32[]{:S(2)}) copy-start(s32[1,1,48]{2,1,0:T(1,128)} %param.12) | copy-start | bytes 580
  0.7 34.4 %copy-start.5 = (bf16[128]{0:T(256)(128)(2,1)S(1)}, bf16[128]{0:T(256)(128)(2,1)}, u32[]{:S(2)}) copy-start(bf16[128]{0:T(256)(128)(2,1)} %param.9) | copy-start | bytes 772
  1.3 1.4 %copy-start = (s32[1,1,48,32,256]{4,3,2,1,0:T(8,128)S(1)}, s32[1,1,48,32,256]{4,3,2,1,0:T(8,128)}, u32[]{:S(2)}) copy-start(s32[1,1,48,32,256]{4,3,2,1,0:T(8,128)} %param.15) | copy-start | bytes 4718596
  2.7 0.8 copy-start.3
  3.5 0.7 copy-start.4
  4.2 30.9 %copy-start.1 = (bf16[128,256]{1,0:T(8,128)(2,1)S(1)}, bf16[128,256]{1,0:T(8,128)(2,1)}, u32[]{:S(2)}) copy-start(bf16[128,256]{1,0:T(8,128)(2,1)} %weight.1) | copy-start | bytes 196612
  4.2 30.9 %copy-start.2 = (bf16[128,256]{1,0:T(8,128)(2,1)S(1)}, bf16[128,256]{1,0:T(8,128)(2,1)}, u32[]{:S(2)}) copy-start(bf16[128,256]{1,0:T(8,128)(2,1)} %cotangent.1) | copy-start | bytes 196612
  31.1 0.7 copy-start.6
  31.8 0.7 copy-start.8
